TPU v7x, 256 devices: a whole 4x4x8 slice. The times are simulated.
256 devices in a mesh: wrap: 256 (over x, z, y, core).
Axes of the slice: x: 4, y: 4, z: 8, core: 2. Of those that a mesh axis runs over, the one named last changes fastest.
Arguments:
- perturbation: float32 [5, 8192, 4, 256], P(None, 'wrap'), may hold values from -6 to 6
- advect_xi: float32 [8192, 256], P('wrap'), may hold values from -1 to 1
- advect_eta: float32 [8192, 256], P('wrap'), may hold values from -0.5 to 0.5
- sponge: float32 [8192, 256], P('wrap'), may hold values from 0.05 to 0.5
- couple_xi: float32 [5, 5], replicated, may hold values from -3 to 3
- couple_eta: float32 [5, 5], replicated, may hold values from -3 to 3
- couple_span: float32 [5, 5], replicated, may hold values from -3 to 3
- wake_cut: int32 [2], replicated, may hold values from 0 to 4096, as said below
- blowing: int32 [8192], P('wrap'), may hold values 0 or 1
Outputs:
- evolved: float32 [5, 8192, 4, 256], P(None, 'wrap')
Inputs may be any that keep to these rules, and one draw needn't show every extreme that they name: wake_cut[0] < wake_cut[1] = 4096.
All inputs are finite; a program needn't handle non-finite values. No bound on the sum of `blowing` on one device may be relied on, other than what follows from the above.
Results may differ from a plain program's by a relative error of at most 0.0003.
Values sent between devices are 32-bit elements; how exact they have to be, the bound alone decides.
No kernel may reach another device: no remote copies, remote signals or barrier semaphores. Data moves between devices by JAX's collectives and lax.ppermute only.
A program may use at most 64 MiB of HBM per device.

v0:
```python
import jax
import jax.numpy as jnp
from jax import lax
from jax.sharding import PartitionSpec as P

STEPS = 2


time_step = 0.2
blow_gain = 1.0


def partner_2(value, axis, distance):
    mask = 2**distance
    pairs = [(source, source ^ mask) for source in range(lax.axis_size(axis))]
    return lax.ppermute(value, axis, pairs)


def extended(cells, sides, width):
    for axis, dim in sides:
        count = lax.axis_size(axis)
        ends = count - 1
        head = lax.slice_in_dim(cells, 0, width, axis=dim)
        tail = lax.slice_in_dim(cells, cells.shape[dim] - width, cells.shape[dim], axis=dim)
        cells = jnp.concatenate(
            [
                lax.ppermute(tail, axis, [(i, (i + 1) % count) for i in range(ends)]),
                cells,
                lax.ppermute(head, axis, [((i + 1) % count, i) for i in range(ends)]),
            ],
            axis=dim,
        )
    return cells


def central(padded, direction, length):

    def shifted(offset):
        return lax.slice_in_dim(padded, 3 + offset, 3 + offset + length, axis=direction)

    return (
        45.0 * (shifted(1) - shifted(-1))
        - 9.0 * (shifted(2) - shifted(-2))
        + (shifted(3) - shifted(-3))
    ) / 60.0


def flip_sign():
    return jnp.array([1.0, 1.0, -1.0, 1.0, 1.0], jnp.float32)[:, None, None, None]


def in_range(values, wake_cut):
    return (values >= wake_cut[0]) & (values < wake_cut[1])


def wall_ghost(wall_strip, wall_pressure, blow_rows, cut_rows, mirror_strip):
    reflected = wall_strip[:, :, :, ::-1] * flip_sign()
    lifted = reflected[2] + 2.0 * blow_gain * blow_rows[:, None, None] * wall_pressure[:, :, None]
    reflected = jnp.concatenate([reflected[:2], lifted[None], reflected[3:]], axis=0)
    mirrored = mirror_strip[:, :, :, ::-1] * flip_sign()
    return jnp.where(cut_rows[None, :, None, None], mirrored, reflected)


def couple(matrix, values):
    return jnp.einsum("cd,dikj->cikj", matrix, values, precision=lax.Precision.HIGHEST)


def linear_rhs(
    values,
    ghost_rows,
    padded_rows,
    advect_xi,
    advect_eta,
    sponge,
    couple_xi,
    couple_eta,
    couple_span,
):
    row_count = values.shape[1]
    normal_count = values.shape[3]
    grad_xi = central(padded_rows, 1, row_count)
    far_field = jnp.zeros(ghost_rows.shape, jnp.float32)
    padded_cols = jnp.concatenate([ghost_rows, values, far_field], axis=3)
    grad_eta = central(padded_cols, 3, normal_count)
    grad_span = (jnp.roll(values, -1, axis=2) - jnp.roll(values, 1, axis=2)) * 0.5
    coef_xi = advect_xi[None, :, None, :]
    coef_eta = advect_eta[None, :, None, :]
    result = -(coef_xi * grad_xi + coef_eta * grad_eta)
    result = (
        result
        - couple(couple_xi, grad_xi)
        - couple(couple_eta, grad_eta)
        - couple(couple_span, grad_span)
    )
    return result - sponge[None, :, None, :] * values


def advance(values, evaluate):
    section_one = values + time_step * evaluate(values)
    section_two = 0.75 * values + 0.25 * (section_one + time_step * evaluate(section_one))
    return values / 3.0 + 2.0 / 3.0 * (section_two + time_step * evaluate(section_two))


def on_device(
    perturbation,
    advect_xi,
    advect_eta,
    sponge,
    couple_xi,
    couple_eta,
    couple_span,
    wake_cut,
    blowing,
):
    row_count = perturbation.shape[1]
    devices = lax.axis_size("wrap")
    position = lax.axis_index("wrap")
    all_rows = row_count * devices
    rows_local = position * row_count + jnp.arange(row_count, dtype=jnp.int32)
    mirror_rows = all_rows - 1 - rows_local
    cut_rows = in_range(rows_local, wake_cut) | in_range(mirror_rows, wake_cut)
    blow_rows = blowing.astype(jnp.float32)

    def partner(wall_strip):
        packed = wall_strip.reshape(wall_strip.shape[0], -1)
        arrived = packed
        for bit_index in range(devices.bit_length() - 1):
            arrived = partner_2(arrived, "wrap", bit_index)
        return arrived.reshape(wall_strip.shape)[:, ::-1]

    def evaluate(values):
        wall_strip = values[:, :, :, :3]
        ghost_rows = wall_ghost(
            wall_strip, values[4, :, :, 0], blow_rows, cut_rows, partner(wall_strip)
        )
        padded_rows = extended(values, (("wrap", 1),), 3)
        return linear_rhs(
            values,
            ghost_rows,
            padded_rows,
            advect_xi,
            advect_eta,
            sponge,
            couple_xi,
            couple_eta,
            couple_span,
        )

    values = perturbation
    for step_index in range(STEPS):
        values = advance(values, evaluate)
    return values


def solution(mesh):
    in_specs = (
        P(None, "wrap", None, None),
        P("wrap", None),
        P("wrap", None),
        P("wrap", None),
        P(),
        P(),
        P(),
        P(),
        P("wrap"),
    )
    out_specs = P(None, "wrap", None, None)
    return jax.shard_map(
        on_device, mesh=mesh, in_specs=in_specs, out_specs=out_specs, check_vma=False
    )
```

profile of v0, /device:TPU:2, one launch (start us, length us, event | category | flops | bytes accessed | tf_op | source)
XLA Modules:
  0.0 328.0 jit_solution(2980378676907527685)
XLA Ops:
  3.3 2.4 collective-permute-start.1
  5.7 9.8 %collective-permute-start = (f32[5,3,4,256]{3,0,2,1:T(8,128)}, f32[5,3,4,256]{3,0,2,1:T(8,128)}, u32[]{:S(2)}, u32[]{:S(2)}) collective-permute-start(f32[5,3,4,256]{3,0,2,1:T(8,128)} %get-tuple-element.39), channel_id=1, source_target_pairs={{1,0},{2,1},{3,2},{4,3},{5,4},{6,5},{7,6},{8,7},{9,8},{10,9},{11,1... | collective-permute-start | bytes 184328 | tf_op jit(solution)/shard_map/ppermute | solution.py:29
  18.6 3.2 collective-permute-done.3
  22.0 5.0 %collective-permute-done.4 = f32[5,384]{1,0:T(8,128)S(1)} collective-permute-done((f32[5,384]{1,0:T(8,128)S(1)}, f32[5,384]{1,0:T(8,128)S(1)}, u32[]{:S(2)}, u32[]{:S(2)}) %collective-permute-start.4) | collective-permute-done | bytes 7712 | tf_op jit(solution)/shard_map/ppermute | solution.py:16
  27.2 3.5 %collective-permute-done.5 = f32[5,384]{1,0:T(8,128)S(1)} collective-permute-done((f32[5,384]{1,0:T(8,128)S(1)}, f32[5,384]{1,0:T(8,128)S(1)}, u32[]{:S(2)}, u32[]{:S(2)}) %collective-permute-start.5) | collective-permute-done | bytes 7712 | tf_op jit(solution)/shard_map/ppermute | solution.py:16
  31.0 4.3 %collective-permute-done.6 = f32[5,384]{1,0:T(8,128)S(1)} collective-permute-done((f32[5,384]{1,0:T(8,128)S(1)}, f32[5,384]{1,0:T(8,128)S(1)}, u32[]{:S(2)}, u32[]{:S(2)}) %collective-permute-start.6) | collective-permute-done | bytes 7712 | tf_op jit(solution)/shard_map/ppermute | solution.py:16
  35.4 3.9 %collective-permute-start.7 = (f32[5,384]{1,0:T(8,128)S(1)}, f32[5,384]{1,0:T(8,128)S(1)}, u32[]{:S(2)}, u32[]{:S(2)}) collective-permute-start(f32[5,384]{1,0:T(8,128)S(1)} %collective-permute-done.6), channel_id=1, source_target_pairs={{0,32},{1,33},{2,34},{3,35},{4,36},{5,37},{6,38},{7,39},{8,40},{9,... | collective-permute-start | bytes 23048 | tf_op jit(solution)/shard_map/ppermute | solution.py:16
  39.2 3.7 %collective-permute-done.7 = f32[5,384]{1,0:T(8,128)S(1)} collective-permute-done((f32[5,384]{1,0:T(8,128)S(1)}, f32[5,384]{1,0:T(8,128)S(1)}, u32[]{:S(2)}, u32[]{:S(2)}) %collective-permute-start.7) | collective-permute-done | bytes 7712 | tf_op jit(solution)/shard_map/ppermute | solution.py:16
  43.6 3.0 collective-permute-done.8
  46.6 2.6 collective-permute-start.9
  57.4 2.0 fusion.138
  60.3 2.1 fusion.43
  68.1 3.8 %collective-permute-done.13 = f32[5,384]{1,0:T(8,128)S(1)} collective-permute-done((f32[5,384]{1,0:T(8,128)}, f32[5,384]{1,0:T(8,128)S(1)}, u32[]{:S(2)}, u32[]{:S(2)}) %collective-permute-start.13) | collective-permute-done | bytes 7712 | tf_op jit(solution)/shard_map/ppermute | solution.py:16
  72.7 4.4 %collective-permute-done.14 = f32[5,384]{1,0:T(8,128)S(1)} collective-permute-done((f32[5,384]{1,0:T(8,128)S(1)}, f32[5,384]{1,0:T(8,128)S(1)}, u32[]{:S(2)}, u32[]{:S(2)}) %collective-permute-start.14) | collective-permute-done | bytes 7712 | tf_op jit(solution)/shard_map/ppermute | solution.py:16
  77.1 3.6 %collective-permute-done.15 = f32[5,384]{1,0:T(8,128)S(1)} collective-permute-done((f32[5,384]{1,0:T(8,128)S(1)}, f32[5,384]{1,0:T(8,128)S(1)}, u32[]{:S(2)}, u32[]{:S(2)}) %collective-permute-start.15) | collective-permute-done | bytes 7712 | tf_op jit(solution)/shard_map/ppermute | solution.py:16
  81.6 3.7 %collective-permute-done.16 = f32[5,384]{1,0:T(8,128)S(1)} collective-permute-done((f32[5,384]{1,0:T(8,128)S(1)}, f32[5,384]{1,0:T(8,128)S(1)}, u32[]{:S(2)}, u32[]{:S(2)}) %collective-permute-start.16) | collective-permute-done | bytes 7712 | tf_op jit(solution)/shard_map/ppermute | solution.py:16
  85.3 3.9 %collective-permute-start.17 = (f32[5,384]{1,0:T(8,128)S(1)}, f32[5,384]{1,0:T(8,128)S(1)}, u32[]{:S(2)}, u32[]{:S(2)}) collective-permute-start(f32[5,384]{1,0:T(8,128)S(1)} %collective-permute-done.16), channel_id=1, source_target_pairs={{0,32},{1,33},{2,34},{3,35},{4,36},{5,37},{6,38},{7,39},{8,40},{9,... | collective-permute-start | bytes 23048 | tf_op jit(solution)/shard_map/ppermute | solution.py:16
  89.3 3.6 %collective-permute-done.17 = f32[5,384]{1,0:T(8,128)S(1)} collective-permute-done((f32[5,384]{1,0:T(8,128)S(1)}, f32[5,384]{1,0:T(8,128)S(1)}, u32[]{:S(2)}, u32[]{:S(2)}) %collective-permute-start.17) | collective-permute-done | bytes 7712 | tf_op jit(solution)/shard_map/ppermute | solution.py:16
  93.4 3.2 collective-permute-done.18
  96.6 2.8 collective-permute-start.19
  101.9 2.4 collective-permute-start.11
  108.8 2.0 fusion.130
  112.3 3.0 fusion.37
  121.2 3.8 %collective-permute-done.23 = f32[5,384]{1,0:T(8,128)S(1)} collective-permute-done((f32[5,384]{1,0:T(8,128)}, f32[5,384]{1,0:T(8,128)S(1)}, u32[]{:S(2)}, u32[]{:S(2)}) %collective-permute-start.23) | collective-permute-done | bytes 7712 | tf_op jit(solution)/shard_map/ppermute | solution.py:16
  125.8 4.4 %collective-permute-done.24 = f32[5,384]{1,0:T(8,128)S(1)} collective-permute-done((f32[5,384]{1,0:T(8,128)S(1)}, f32[5,384]{1,0:T(8,128)S(1)}, u32[]{:S(2)}, u32[]{:S(2)}) %collective-permute-start.24) | collective-permute-done | bytes 7712 | tf_op jit(solution)/shard_map/ppermute | solution.py:16
  130.2 3.6 %collective-permute-done.25 = f32[5,384]{1,0:T(8,128)S(1)} collective-permute-done((f32[5,384]{1,0:T(8,128)S(1)}, f32[5,384]{1,0:T(8,128)S(1)}, u32[]{:S(2)}, u32[]{:S(2)}) %collective-permute-start.25) | collective-permute-done | bytes 7712 | tf_op jit(solution)/shard_map/ppermute | solution.py:16
  134.7 3.7 %collective-permute-done.26 = f32[5,384]{1,0:T(8,128)S(1)} collective-permute-done((f32[5,384]{1,0:T(8,128)S(1)}, f32[5,384]{1,0:T(8,128)S(1)}, u32[]{:S(2)}, u32[]{:S(2)}) %collective-permute-start.26) | collective-permute-done | bytes 7712 | tf_op jit(solution)/shard_map/ppermute | solution.py:16
  138.4 2.9 collective-permute-start.27
  141.5 4.7 %collective-permute-done.27 = f32[5,384]{1,0:T(8,128)S(1)} collective-permute-done((f32[5,384]{1,0:T(8,128)S(1)}, f32[5,384]{1,0:T(8,128)S(1)}, u32[]{:S(2)}, u32[]{:S(2)}) %collective-permute-start.27) | collective-permute-done | bytes 7712 | tf_op jit(solution)/shard_map/ppermute | solution.py:16
  146.6 3.2 collective-permute-done.28
  153.4 2.4 collective-permute-start.21
  160.3 2.0 fusion.122
  163.9 3.0 fusion.29
  172.3 3.5 %collective-permute-done.33 = f32[5,384]{1,0:T(8,128)S(1)} collective-permute-done((f32[5,384]{1,0:T(8,128)S(1)}, f32[5,384]{1,0:T(8,128)S(1)}, u32[]{:S(2)}, u32[]{:S(2)}) %collective-permute-start.33) | collective-permute-done | bytes 7712 | tf_op jit(solution)/shard_map/ppermute | solution.py:16
  176.8 4.3 %collective-permute-done.34 = f32[5,384]{1,0:T(8,128)S(1)} collective-permute-done((f32[5,384]{1,0:T(8,128)S(1)}, f32[5,384]{1,0:T(8,128)S(1)}, u32[]{:S(2)}, u32[]{:S(2)}) %collective-permute-start.34) | collective-permute-done | bytes 7712 | tf_op jit(solution)/shard_map/ppermute | solution.py:16
  181.6 3.6 %collective-permute-done.35 = f32[5,384]{1,0:T(8,128)S(1)} collective-permute-done((f32[5,384]{1,0:T(8,128)S(1)}, f32[5,384]{1,0:T(8,128)S(1)}, u32[]{:S(2)}, u32[]{:S(2)}) %collective-permute-start.35) | collective-permute-done | bytes 7712 | tf_op jit(solution)/shard_map/ppermute | solution.py:16
  185.4 4.4 %collective-permute-done.36 = f32[5,384]{1,0:T(8,128)S(1)} collective-permute-done((f32[5,384]{1,0:T(8,128)S(1)}, f32[5,384]{1,0:T(8,128)S(1)}, u32[]{:S(2)}, u32[]{:S(2)}) %collective-permute-start.36) | collective-permute-done | bytes 7712 | tf_op jit(solution)/shard_map/ppermute | solution.py:16
  189.8 2.2 collective-permute-start.37
  192.2 5.2 %collective-permute-done.37 = f32[5,384]{1,0:T(8,128)S(1)} collective-permute-done((f32[5,384]{1,0:T(8,128)S(1)}, f32[5,384]{1,0:T(8,128)S(1)}, u32[]{:S(2)}, u32[]{:S(2)}) %collective-permute-start.37) | collective-permute-done | bytes 7712 | tf_op jit(solution)/shard_map/ppermute | solution.py:16
  197.6 3.4 %collective-permute-done.38 = f32[5,384]{1,0:T(8,128)S(1)} collective-permute-done((f32[5,384]{1,0:T(8,128)S(1)}, f32[5,384]{1,0:T(8,128)S(1)}, u32[]{:S(2)}, u32[]{:S(2)}) %collective-permute-start.38) | collective-permute-done | bytes 7712 | tf_op jit(solution)/shard_map/ppermute | solution.py:16
  201.1 2.4 collective-permute-start.39
  205.9 2.4 collective-permute-start.31
  209.3 2.0 fusion.114
  211.9 4.3 %collective-permute-done.31 = f32[5,3,4,256]{3,0,2,1:T(8,128)} collective-permute-done((f32[5,3,4,256]{3,0,2,1:T(8,128)S(1)}, f32[5,3,4,256]{3,0,2,1:T(8,128)}, u32[]{:S(2)}, u32[]{:S(2)}) %collective-permute-start.31) | collective-permute-done | bytes 61472 | tf_op jit(solution)/shard_map/ppermute | solution.py:27
  216.2 3.1 fusion.21
  224.4 3.5 %collective-permute-done.43 = f32[5,384]{1,0:T(8,128)S(1)} collective-permute-done((f32[5,384]{1,0:T(8,128)S(1)}, f32[5,384]{1,0:T(8,128)S(1)}, u32[]{:S(2)}, u32[]{:S(2)}) %collective-permute-start.43) | collective-permute-done | bytes 7712 | tf_op jit(solution)/shard_map/ppermute | solution.py:16
  229.0 4.4 %collective-permute-done.44 = f32[5,384]{1,0:T(8,128)S(1)} collective-permute-done((f32[5,384]{1,0:T(8,128)S(1)}, f32[5,384]{1,0:T(8,128)S(1)}, u32[]{:S(2)}, u32[]{:S(2)}) %collective-permute-start.44) | collective-permute-done | bytes 7712 | tf_op jit(solution)/shard_map/ppermute | solution.py:16
  233.4 3.6 %collective-permute-done.45 = f32[5,384]{1,0:T(8,128)S(1)} collective-permute-done((f32[5,384]{1,0:T(8,128)S(1)}, f32[5,384]{1,0:T(8,128)S(1)}, u32[]{:S(2)}, u32[]{:S(2)}) %collective-permute-start.45) | collective-permute-done | bytes 7712 | tf_op jit(solution)/shard_map/ppermute | solution.py:16
  237.9 3.7 %collective-permute-done.46 = f32[5,384]{1,0:T(8,128)S(1)} collective-permute-done((f32[5,384]{1,0:T(8,128)S(1)}, f32[5,384]{1,0:T(8,128)S(1)}, u32[]{:S(2)}, u32[]{:S(2)}) %collective-permute-start.46) | collective-permute-done | bytes 7712 | tf_op jit(solution)/shard_map/ppermute | solution.py:16
  242.7 6.5 %collective-permute-done.47 = f32[5,384]{1,0:T(8,128)S(1)} collective-permute-done((f32[5,384]{1,0:T(8,128)S(1)}, f32[5,384]{1,0:T(8,128)S(1)}, u32[]{:S(2)}, u32[]{:S(2)}) %collective-permute-start.47) | collective-permute-done | bytes 7712 | tf_op jit(solution)/shard_map/ppermute | solution.py:16
  249.5 3.4 %collective-permute-done.48 = f32[5,384]{1,0:T(8,128)S(1)} collective-permute-done((f32[5,384]{1,0:T(8,128)S(1)}, f32[5,384]{1,0:T(8,128)S(1)}, u32[]{:S(2)}, u32[]{:S(2)}) %collective-permute-start.48) | collective-permute-done | bytes 7712 | tf_op jit(solution)/shard_map/ppermute | solution.py:16
  256.5 2.4 collective-permute-start.41
  261.7 2.0 fusion.106
  263.7 3.3 collective-permute-done.41
  267.0 3.1 fusion.15
  277.1 2.5 collective-permute-done.53
  280.4 4.3 %collective-permute-done.54 = f32[5,384]{1,0:T(8,128)S(1)} collective-permute-done((f32[5,384]{1,0:T(8,128)S(1)}, f32[5,384]{1,0:T(8,128)S(1)}, u32[]{:S(2)}, u32[]{:S(2)}) %collective-permute-start.54) | collective-permute-done | bytes 7712 | tf_op jit(solution)/shard_map/ppermute | solution.py:16
  285.6 2.9 collective-permute-done.55
  289.3 3.8 %collective-permute-done.56 = f32[5,384]{1,0:T(8,128)} collective-permute-done((f32[5,384]{1,0:T(8,128)S(1)}, f32[5,384]{1,0:T(8,128)}, u32[]{:S(2)}, u32[]{:S(2)}) %collective-permute-start.56) | collective-permute-done | bytes 7712 | tf_op jit(solution)/shard_map/ppermute | solution.py:16
  293.9 7.1 %collective-permute-done.57 = f32[5,384]{1,0:T(8,128)S(1)} collective-permute-done((f32[5,384]{1,0:T(8,128)}, f32[5,384]{1,0:T(8,128)S(1)}, u32[]{:S(2)}, u32[]{:S(2)}) %collective-permute-start.57) | collective-permute-done | bytes 7712 | tf_op jit(solution)/shard_map/ppermute | solution.py:16
  304.7 2.4 collective-permute-start.59
  308.4 2.0 collective-permute-start.50
  310.4 2.4 collective-permute-start.51
  320.9 3.0 fusion.7
  (339 shorter events, 103.5 us)
Async XLA Ops:
  0.0 60.3 %copy-start = (f32[5,5]{1,0:T(8,128)S(1)}, f32[5,5]{1,0:T(8,128)}, u32[]{:S(2)}) copy-start(f32[5,5]{1,0:T(8,128)} %param.25) | copy-start | bytes 304
  2.6 15.3 %collective-permute-start.2 = (f32[5,384]{1,0:T(8,128)}, f32[5,384]{1,0:T(8,128)}, u32[]{:S(2)}, u32[]{:S(2)}) collective-permute-start(f32[5,384]{1,0:T(8,128)} %reshape.188), channel_id=1, source_target_pairs={{0,1},{1,0},{2,3},{3,2},{4,5},{5,4},{6,7},{7,6},{8,9},{9,8},{10,11... | collective-permute-start | bytes 23048 | tf_op jit(solution)/shard_map/ppermute | solution.py:16
  3.3 52.0 %collective-permute-start.1 = (f32[5,3,4,256]{3,0,2,1:T(8,128)}, f32[5,3,4,256]{3,0,2,1:T(8,128)}, u32[]{:S(2)}, u32[]{:S(2)}) collective-permute-start(f32[5,3,4,256]{3,0,2,1:T(8,128)} %get-tuple-element.40), channel_id=1, source_target_pairs={{0,1},{1,2},{2,3},{3,4},{4,5},{5,6},{6,7},{7,8},{8,9},{9,10},{10,1... | collective-permute-start | bytes 184328 | tf_op jit(solution)/shard_map/ppermute | solution.py:27
  5.7 53.6 %collective-permute-start = (f32[5,3,4,256]{3,0,2,1:T(8,128)}, f32[5,3,4,256]{3,0,2,1:T(8,128)}, u32[]{:S(2)}, u32[]{:S(2)}) collective-permute-start(f32[5,3,4,256]{3,0,2,1:T(8,128)} %get-tuple-element.39), channel_id=1, source_target_pairs={{1,0},{2,1},{3,2},{4,3},{5,4},{6,5},{7,6},{8,7},{9,8},{10,9},{11,1... | collective-permute-start | bytes 184328 | tf_op jit(solution)/shard_map/ppermute | solution.py:29
  17.7 25.2 %copy-start.53 = (s32[2]{0:T(128)S(1)}, s32[2]{0:T(128)}, u32[]{:S(2)}) copy-start(s32[2]{0:T(128)} %param.28) | copy-start | bytes 28
  17.9 4.0 %collective-permute-start.3 = (f32[5,384]{1,0:T(8,128)}, f32[5,384]{1,0:T(8,128)S(1)}, u32[]{:S(2)}, u32[]{:S(2)}) collective-permute-start(f32[5,384]{1,0:T(8,128)} %collective-permute-done.2), channel_id=1, source_target_pairs={{0,2},{1,3},{2,0},{3,1},{4,6},{5,7},{6,4},{7,5},{8,10},{9,11},{10,... | collective-permute-start | bytes 23048 | tf_op jit(solution)/shard_map/ppermute | solution.py:16
  21.9 5.2 %collective-permute-start.4 = (f32[5,384]{1,0:T(8,128)S(1)}, f32[5,384]{1,0:T(8,128)S(1)}, u32[]{:S(2)}, u32[]{:S(2)}) collective-permute-start(f32[5,384]{1,0:T(8,128)S(1)} %collective-permute-done.3), channel_id=1, source_target_pairs={{0,4},{1,5},{2,6},{3,7},{4,0},{5,1},{6,2},{7,3},{8,12},{9,13},{10,... | collective-permute-start | bytes 23048 | tf_op jit(solution)/shard_map/ppermute | solution.py:16
  27.1 3.7 %collective-permute-start.5 = (f32[5,384]{1,0:T(8,128)S(1)}, f32[5,384]{1,0:T(8,128)S(1)}, u32[]{:S(2)}, u32[]{:S(2)}) collective-permute-start(f32[5,384]{1,0:T(8,128)S(1)} %collective-permute-done.4), channel_id=1, source_target_pairs={{0,8},{1,9},{2,10},{3,11},{4,12},{5,13},{6,14},{7,15},{8,0},{9,1},... | collective-permute-start | bytes 23048 | tf_op jit(solution)/shard_map/ppermute | solution.py:16
  30.8 4.6 %collective-permute-start.6 = (f32[5,384]{1,0:T(8,128)S(1)}, f32[5,384]{1,0:T(8,128)S(1)}, u32[]{:S(2)}, u32[]{:S(2)}) collective-permute-start(f32[5,384]{1,0:T(8,128)S(1)} %collective-permute-done.5), channel_id=1, source_target_pairs={{0,16},{1,17},{2,18},{3,19},{4,20},{5,21},{6,22},{7,23},{8,24},{9,... | collective-permute-start | bytes 23048 | tf_op jit(solution)/shard_map/ppermute | solution.py:16
  35.4 7.6 %collective-permute-start.7 = (f32[5,384]{1,0:T(8,128)S(1)}, f32[5,384]{1,0:T(8,128)S(1)}, u32[]{:S(2)}, u32[]{:S(2)}) collective-permute-start(f32[5,384]{1,0:T(8,128)S(1)} %collective-permute-done.6), channel_id=1, source_target_pairs={{0,32},{1,33},{2,34},{3,35},{4,36},{5,37},{6,38},{7,39},{8,40},{9,... | collective-permute-start | bytes 23048 | tf_op jit(solution)/shard_map/ppermute | solution.py:16
  43.0 3.7 %collective-permute-start.8 = (f32[5,384]{1,0:T(8,128)S(1)}, f32[5,384]{1,0:T(8,128)S(1)}, u32[]{:S(2)}, u32[]{:S(2)}) collective-permute-start(f32[5,384]{1,0:T(8,128)S(1)} %collective-permute-done.7), channel_id=1, source_target_pairs={{0,64},{1,65},{2,66},{3,67},{4,68},{5,69},{6,70},{7,71},{8,72},{9,... | collective-permute-start | bytes 23048 | tf_op jit(solution)/shard_map/ppermute | solution.py:16
  46.6 5.4 %collective-permute-start.9 = (f32[5,384]{1,0:T(8,128)S(1)}, f32[5,384]{1,0:T(8,128)S(1)}, u32[]{:S(2)}, u32[]{:S(2)}) collective-permute-start(f32[5,384]{1,0:T(8,128)S(1)} %collective-permute-done.8), channel_id=1, source_target_pairs={{0,128},{1,129},{2,130},{3,131},{4,132},{5,133},{6,134},{7,135},{8... | collective-permute-start | bytes 23048 | tf_op jit(solution)/shard_map/ppermute | solution.py:16
  66.4 1.5 collective-permute-start.12
  67.9 3.9 %collective-permute-start.13 = (f32[5,384]{1,0:T(8,128)}, f32[5,384]{1,0:T(8,128)S(1)}, u32[]{:S(2)}, u32[]{:S(2)}) collective-permute-start(f32[5,384]{1,0:T(8,128)} %collective-permute-done.12), channel_id=1, source_target_pairs={{0,2},{1,3},{2,0},{3,1},{4,6},{5,7},{6,4},{7,5},{8,10},{9,11},{10,... | collective-permute-start | bytes 23048 | tf_op jit(solution)/shard_map/ppermute | solution.py:16
  68.0 21.1 %copy-start.48 = (f32[32]{0:T(128)S(1)}, f32[32]{0:T(128)}, u32[]{:S(2)}) copy-start(f32[32]{0:T(128)} %copy-done.47) | copy-start | bytes 388
  71.8 5.2 %collective-permute-start.14 = (f32[5,384]{1,0:T(8,128)S(1)}, f32[5,384]{1,0:T(8,128)S(1)}, u32[]{:S(2)}, u32[]{:S(2)}) collective-permute-start(f32[5,384]{1,0:T(8,128)S(1)} %collective-permute-done.13), channel_id=1, source_target_pairs={{0,4},{1,5},{2,6},{3,7},{4,0},{5,1},{6,2},{7,3},{8,12},{9,13},{10,... | collective-permute-start | bytes 23048 | tf_op jit(solution)/shard_map/ppermute | solution.py:16
  77.0 3.7 %collective-permute-start.15 = (f32[5,384]{1,0:T(8,128)S(1)}, f32[5,384]{1,0:T(8,128)S(1)}, u32[]{:S(2)}, u32[]{:S(2)}) collective-permute-start(f32[5,384]{1,0:T(8,128)S(1)} %collective-permute-done.14), channel_id=1, source_target_pairs={{0,8},{1,9},{2,10},{3,11},{4,12},{5,13},{6,14},{7,15},{8,0},{9,1},... | collective-permute-start | bytes 23048 | tf_op jit(solution)/shard_map/ppermute | solution.py:16
  80.7 4.6 %collective-permute-start.16 = (f32[5,384]{1,0:T(8,128)S(1)}, f32[5,384]{1,0:T(8,128)S(1)}, u32[]{:S(2)}, u32[]{:S(2)}) collective-permute-start(f32[5,384]{1,0:T(8,128)S(1)} %collective-permute-done.15), channel_id=1, source_target_pairs={{0,16},{1,17},{2,18},{3,19},{4,20},{5,21},{6,22},{7,23},{8,24},{9,... | collective-permute-start | bytes 23048 | tf_op jit(solution)/shard_map/ppermute | solution.py:16
  85.3 7.6 %collective-permute-start.17 = (f32[5,384]{1,0:T(8,128)S(1)}, f32[5,384]{1,0:T(8,128)S(1)}, u32[]{:S(2)}, u32[]{:S(2)}) collective-permute-start(f32[5,384]{1,0:T(8,128)S(1)} %collective-permute-done.16), channel_id=1, source_target_pairs={{0,32},{1,33},{2,34},{3,35},{4,36},{5,37},{6,38},{7,39},{8,40},{9,... | collective-permute-start | bytes 23048 | tf_op jit(solution)/shard_map/ppermute | solution.py:16
  92.9 3.7 %collective-permute-start.18 = (f32[5,384]{1,0:T(8,128)S(1)}, f32[5,384]{1,0:T(8,128)S(1)}, u32[]{:S(2)}, u32[]{:S(2)}) collective-permute-start(f32[5,384]{1,0:T(8,128)S(1)} %collective-permute-done.17), channel_id=1, source_target_pairs={{0,64},{1,65},{2,66},{3,67},{4,68},{5,69},{6,70},{7,71},{8,72},{9,... | collective-permute-start | bytes 23048 | tf_op jit(solution)/shard_map/ppermute | solution.py:16
  96.6 7.7 %collective-permute-start.19 = (f32[5,384]{1,0:T(8,128)S(1)}, f32[5,384]{1,0:T(8,128)S(1)}, u32[]{:S(2)}, u32[]{:S(2)}) collective-permute-start(f32[5,384]{1,0:T(8,128)S(1)} %collective-permute-done.18), channel_id=1, source_target_pairs={{0,128},{1,129},{2,130},{3,131},{4,132},{5,133},{6,134},{7,135},{8... | collective-permute-start | bytes 23048 | tf_op jit(solution)/shard_map/ppermute | solution.py:16
  99.9 10.8 %collective-permute-start.10 = (f32[5,3,4,256]{3,0,2,1:T(8,128)}, f32[5,3,4,256]{3,0,2,1:T(8,128)}, u32[]{:S(2)}, u32[]{:S(2)}) collective-permute-start(f32[5,3,4,256]{3,0,2,1:T(8,128)} %get-tuple-element.33), channel_id=1, source_target_pairs={{1,0},{2,1},{3,2},{4,3},{5,4},{6,5},{7,6},{8,7},{9,8},{10,9},{11,1... | collective-permute-start | bytes 184328 | tf_op jit(solution)/shard_map/ppermute | solution.py:29
  101.9 10.5 %collective-permute-start.11 = (f32[5,3,4,256]{3,0,2,1:T(8,128)}, f32[5,3,4,256]{3,0,2,1:T(8,128)}, u32[]{:S(2)}, u32[]{:S(2)}) collective-permute-start(f32[5,3,4,256]{3,0,2,1:T(8,128)} %get-tuple-element.34), channel_id=1, source_target_pairs={{0,1},{1,2},{2,3},{3,4},{4,5},{5,6},{6,7},{7,8},{8,9},{9,10},{10,1... | collective-permute-start | bytes 184328 | tf_op jit(solution)/shard_map/ppermute | solution.py:27
  119.5 1.5 collective-permute-start.22
  121.0 3.9 %collective-permute-start.23 = (f32[5,384]{1,0:T(8,128)}, f32[5,384]{1,0:T(8,128)S(1)}, u32[]{:S(2)}, u32[]{:S(2)}) collective-permute-start(f32[5,384]{1,0:T(8,128)} %collective-permute-done.22), channel_id=1, source_target_pairs={{0,2},{1,3},{2,0},{3,1},{4,6},{5,7},{6,4},{7,5},{8,10},{9,11},{10,... | collective-permute-start | bytes 23048 | tf_op jit(solution)/shard_map/ppermute | solution.py:16
  121.1 20.2 %copy-start.49 = (f32[32]{0:T(128)S(1)}, f32[32]{0:T(128)}, u32[]{:S(2)}) copy-start(f32[32]{0:T(128)} %copy-done.47) | copy-start | bytes 388
  124.9 5.2 %collective-permute-start.24 = (f32[5,384]{1,0:T(8,128)S(1)}, f32[5,384]{1,0:T(8,128)S(1)}, u32[]{:S(2)}, u32[]{:S(2)}) collective-permute-start(f32[5,384]{1,0:T(8,128)S(1)} %collective-permute-done.23), channel_id=1, source_target_pairs={{0,4},{1,5},{2,6},{3,7},{4,0},{5,1},{6,2},{7,3},{8,12},{9,13},{10,... | collective-permute-start | bytes 23048 | tf_op jit(solution)/shard_map/ppermute | solution.py:16
  130.1 3.7 %collective-permute-start.25 = (f32[5,384]{1,0:T(8,128)S(1)}, f32[5,384]{1,0:T(8,128)S(1)}, u32[]{:S(2)}, u32[]{:S(2)}) collective-permute-start(f32[5,384]{1,0:T(8,128)S(1)} %collective-permute-done.24), channel_id=1, source_target_pairs={{0,8},{1,9},{2,10},{3,11},{4,12},{5,13},{6,14},{7,15},{8,0},{9,1},... | collective-permute-start | bytes 23048 | tf_op jit(solution)/shard_map/ppermute | solution.py:16
  133.8 4.6 %collective-permute-start.26 = (f32[5,384]{1,0:T(8,128)S(1)}, f32[5,384]{1,0:T(8,128)S(1)}, u32[]{:S(2)}, u32[]{:S(2)}) collective-permute-start(f32[5,384]{1,0:T(8,128)S(1)} %collective-permute-done.25), channel_id=1, source_target_pairs={{0,16},{1,17},{2,18},{3,19},{4,20},{5,21},{6,22},{7,23},{8,24},{9,... | collective-permute-start | bytes 23048 | tf_op jit(solution)/shard_map/ppermute | solution.py:16
  138.4 7.8 %collective-permute-start.27 = (f32[5,384]{1,0:T(8,128)S(1)}, f32[5,384]{1,0:T(8,128)S(1)}, u32[]{:S(2)}, u32[]{:S(2)}) collective-permute-start(f32[5,384]{1,0:T(8,128)S(1)} %collective-permute-done.26), channel_id=1, source_target_pairs={{0,32},{1,33},{2,34},{3,35},{4,36},{5,37},{6,38},{7,39},{8,40},{9,... | collective-permute-start | bytes 23048 | tf_op jit(solution)/shard_map/ppermute | solution.py:16
  146.2 3.7 %collective-permute-start.28 = (f32[5,384]{1,0:T(8,128)S(1)}, f32[5,384]{1,0:T(8,128)S(1)}, u32[]{:S(2)}, u32[]{:S(2)}) collective-permute-start(f32[5,384]{1,0:T(8,128)S(1)} %collective-permute-done.27), channel_id=1, source_target_pairs={{0,64},{1,65},{2,66},{3,67},{4,68},{5,69},{6,70},{7,71},{8,72},{9,... | collective-permute-start | bytes 23048 | tf_op jit(solution)/shard_map/ppermute | solution.py:16
  149.9 6.0 %collective-permute-start.29 = (f32[5,384]{1,0:T(8,128)S(1)}, f32[5,384]{1,0:T(8,128)S(1)}, u32[]{:S(2)}, u32[]{:S(2)}) collective-permute-start(f32[5,384]{1,0:T(8,128)S(1)} %collective-permute-done.28), channel_id=1, source_target_pairs={{0,128},{1,129},{2,130},{3,131},{4,132},{5,133},{6,134},{7,135},{8... | collective-permute-start | bytes 23048 | tf_op jit(solution)/shard_map/ppermute | solution.py:16
  151.5 10.8 %collective-permute-start.20 = (f32[5,3,4,256]{3,0,2,1:T(8,128)}, f32[5,3,4,256]{3,0,2,1:T(8,128)}, u32[]{:S(2)}, u32[]{:S(2)}) collective-permute-start(f32[5,3,4,256]{3,0,2,1:T(8,128)} %get-tuple-element.27), channel_id=1, source_target_pairs={{1,0},{2,1},{3,2},{4,3},{5,4},{6,5},{7,6},{8,7},{9,8},{10,9},{11,1... | collective-permute-start | bytes 184328 | tf_op jit(solution)/shard_map/ppermute | solution.py:29
  153.4 10.5 %collective-permute-start.21 = (f32[5,3,4,256]{3,0,2,1:T(8,128)}, f32[5,3,4,256]{3,0,2,1:T(8,128)}, u32[]{:S(2)}, u32[]{:S(2)}) collective-permute-start(f32[5,3,4,256]{3,0,2,1:T(8,128)} %get-tuple-element.28), channel_id=1, source_target_pairs={{0,1},{1,2},{2,3},{3,4},{4,5},{5,6},{6,7},{7,8},{8,9},{9,10},{10,1... | collective-permute-start | bytes 184328 | tf_op jit(solution)/shard_map/ppermute | solution.py:27
  170.5 1.6 collective-permute-start.32
  172.1 3.8 %collective-permute-start.33 = (f32[5,384]{1,0:T(8,128)S(1)}, f32[5,384]{1,0:T(8,128)S(1)}, u32[]{:S(2)}, u32[]{:S(2)}) collective-permute-start(f32[5,384]{1,0:T(8,128)S(1)} %collective-permute-done.32), channel_id=1, source_target_pairs={{0,2},{1,3},{2,0},{3,1},{4,6},{5,7},{6,4},{7,5},{8,10},{9,11},{10,... | collective-permute-start | bytes 23048 | tf_op jit(solution)/shard_map/ppermute | solution.py:16
  175.9 5.2 %collective-permute-start.34 = (f32[5,384]{1,0:T(8,128)S(1)}, f32[5,384]{1,0:T(8,128)S(1)}, u32[]{:S(2)}, u32[]{:S(2)}) collective-permute-start(f32[5,384]{1,0:T(8,128)S(1)} %collective-permute-done.33), channel_id=1, source_target_pairs={{0,4},{1,5},{2,6},{3,7},{4,0},{5,1},{6,2},{7,3},{8,12},{9,13},{10,... | collective-permute-start | bytes 23048 | tf_op jit(solution)/shard_map/ppermute | solution.py:16
  181.1 4.1 %collective-permute-start.35 = (f32[5,384]{1,0:T(8,128)S(1)}, f32[5,384]{1,0:T(8,128)S(1)}, u32[]{:S(2)}, u32[]{:S(2)}) collective-permute-start(f32[5,384]{1,0:T(8,128)S(1)} %collective-permute-done.34), channel_id=1, source_target_pairs={{0,8},{1,9},{2,10},{3,11},{4,12},{5,13},{6,14},{7,15},{8,0},{9,1},... | collective-permute-start | bytes 23048 | tf_op jit(solution)/shard_map/ppermute | solution.py:16
  185.2 4.6 %collective-permute-start.36 = (f32[5,384]{1,0:T(8,128)S(1)}, f32[5,384]{1,0:T(8,128)S(1)}, u32[]{:S(2)}, u32[]{:S(2)}) collective-permute-start(f32[5,384]{1,0:T(8,128)S(1)} %collective-permute-done.35), channel_id=1, source_target_pairs={{0,16},{1,17},{2,18},{3,19},{4,20},{5,21},{6,22},{7,23},{8,24},{9,... | collective-permute-start | bytes 23048 | tf_op jit(solution)/shard_map/ppermute | solution.py:16
  189.8 7.6 %collective-permute-start.37 = (f32[5,384]{1,0:T(8,128)S(1)}, f32[5,384]{1,0:T(8,128)S(1)}, u32[]{:S(2)}, u32[]{:S(2)}) collective-permute-start(f32[5,384]{1,0:T(8,128)S(1)} %collective-permute-done.36), channel_id=1, source_target_pairs={{0,32},{1,33},{2,34},{3,35},{4,36},{5,37},{6,38},{7,39},{8,40},{9,... | collective-permute-start | bytes 23048 | tf_op jit(solution)/shard_map/ppermute | solution.py:16
  197.4 3.7 %collective-permute-start.38 = (f32[5,384]{1,0:T(8,128)S(1)}, f32[5,384]{1,0:T(8,128)S(1)}, u32[]{:S(2)}, u32[]{:S(2)}) collective-permute-start(f32[5,384]{1,0:T(8,128)S(1)} %collective-permute-done.37), channel_id=1, source_target_pairs={{0,64},{1,65},{2,66},{3,67},{4,68},{5,69},{6,70},{7,71},{8,72},{9,... | collective-permute-start | bytes 23048 | tf_op jit(solution)/shard_map/ppermute | solution.py:16
  201.1 7.3 %collective-permute-start.39 = (f32[5,384]{1,0:T(8,128)S(1)}, f32[5,384]{1,0:T(8,128)S(1)}, u32[]{:S(2)}, u32[]{:S(2)}) collective-permute-start(f32[5,384]{1,0:T(8,128)S(1)} %collective-permute-done.38), channel_id=1, source_target_pairs={{0,128},{1,129},{2,130},{3,131},{4,132},{5,133},{6,134},{7,135},{8... | collective-permute-start | bytes 23048 | tf_op jit(solution)/shard_map/ppermute | solution.py:16
  204.0 7.3 %collective-permute-start.30 = (f32[5,3,4,256]{3,0,2,1:T(8,128)S(1)}, f32[5,3,4,256]{3,0,2,1:T(8,128)S(1)}, u32[]{:S(2)}, u32[]{:S(2)}) collective-permute-start(f32[5,3,4,256]{3,0,2,1:T(8,128)S(1)} %get-tuple-element.21), channel_id=1, source_target_pairs={{1,0},{2,1},{3,2},{4,3},{5,4},{6,5},{7,6},{8,7},{9,8},{10,9},{11,1... | collective-permute-start | bytes 184328 | tf_op jit(solution)/shard_map/ppermute | solution.py:29
  205.9 10.3 %collective-permute-start.31 = (f32[5,3,4,256]{3,0,2,1:T(8,128)S(1)}, f32[5,3,4,256]{3,0,2,1:T(8,128)}, u32[]{:S(2)}, u32[]{:S(2)}) collective-permute-start(f32[5,3,4,256]{3,0,2,1:T(8,128)S(1)} %get-tuple-element.22), channel_id=1, source_target_pairs={{0,1},{1,2},{2,3},{3,4},{4,5},{5,6},{6,7},{7,8},{8,9},{9,10},{10,1... | collective-permute-start | bytes 184328 | tf_op jit(solution)/shard_map/ppermute | solution.py:27
  222.6 1.6 collective-permute-start.42
  224.2 3.8 %collective-permute-start.43 = (f32[5,384]{1,0:T(8,128)S(1)}, f32[5,384]{1,0:T(8,128)S(1)}, u32[]{:S(2)}, u32[]{:S(2)}) collective-permute-start(f32[5,384]{1,0:T(8,128)S(1)} %collective-permute-done.42), channel_id=1, source_target_pairs={{0,2},{1,3},{2,0},{3,1},{4,6},{5,7},{6,4},{7,5},{8,10},{9,11},{10,... | collective-permute-start | bytes 23048 | tf_op jit(solution)/shard_map/ppermute | solution.py:16
  228.0 5.3 %collective-permute-start.44 = (f32[5,384]{1,0:T(8,128)S(1)}, f32[5,384]{1,0:T(8,128)S(1)}, u32[]{:S(2)}, u32[]{:S(2)}) collective-permute-start(f32[5,384]{1,0:T(8,128)S(1)} %collective-permute-done.43), channel_id=1, source_target_pairs={{0,4},{1,5},{2,6},{3,7},{4,0},{5,1},{6,2},{7,3},{8,12},{9,13},{10,... | collective-permute-start | bytes 23048 | tf_op jit(solution)/shard_map/ppermute | solution.py:16
  233.3 3.7 %collective-permute-start.45 = (f32[5,384]{1,0:T(8,128)S(1)}, f32[5,384]{1,0:T(8,128)S(1)}, u32[]{:S(2)}, u32[]{:S(2)}) collective-permute-start(f32[5,384]{1,0:T(8,128)S(1)} %collective-permute-done.44), channel_id=1, source_target_pairs={{0,8},{1,9},{2,10},{3,11},{4,12},{5,13},{6,14},{7,15},{8,0},{9,1},... | collective-permute-start | bytes 23048 | tf_op jit(solution)/shard_map/ppermute | solution.py:16
  237.0 4.6 %collective-permute-start.46 = (f32[5,384]{1,0:T(8,128)S(1)}, f32[5,384]{1,0:T(8,128)S(1)}, u32[]{:S(2)}, u32[]{:S(2)}) collective-permute-start(f32[5,384]{1,0:T(8,128)S(1)} %collective-permute-done.45), channel_id=1, source_target_pairs={{0,16},{1,17},{2,18},{3,19},{4,20},{5,21},{6,22},{7,23},{8,24},{9,... | collective-permute-start | bytes 23048 | tf_op jit(solution)/shard_map/ppermute | solution.py:16
  241.6 7.6 %collective-permute-start.47 = (f32[5,384]{1,0:T(8,128)S(1)}, f32[5,384]{1,0:T(8,128)S(1)}, u32[]{:S(2)}, u32[]{:S(2)}) collective-permute-start(f32[5,384]{1,0:T(8,128)S(1)} %collective-permute-done.46), channel_id=1, source_target_pairs={{0,32},{1,33},{2,34},{3,35},{4,36},{5,37},{6,38},{7,39},{8,40},{9,... | collective-permute-start | bytes 23048 | tf_op jit(solution)/shard_map/ppermute | solution.py:16
  249.2 3.7 %collective-permute-start.48 = (f32[5,384]{1,0:T(8,128)S(1)}, f32[5,384]{1,0:T(8,128)S(1)}, u32[]{:S(2)}, u32[]{:S(2)}) collective-permute-start(f32[5,384]{1,0:T(8,128)S(1)} %collective-permute-done.47), channel_id=1, source_target_pairs={{0,64},{1,65},{2,66},{3,67},{4,68},{5,69},{6,70},{7,71},{8,72},{9,... | collective-permute-start | bytes 23048 | tf_op jit(solution)/shard_map/ppermute | solution.py:16
  252.9 6.0 %collective-permute-start.49 = (f32[5,384]{1,0:T(8,128)S(1)}, f32[5,384]{1,0:T(8,128)S(1)}, u32[]{:S(2)}, u32[]{:S(2)}) collective-permute-start(f32[5,384]{1,0:T(8,128)S(1)} %collective-permute-done.48), channel_id=1, source_target_pairs={{0,128},{1,129},{2,130},{3,131},{4,132},{5,133},{6,134},{7,135},{8... | collective-permute-start | bytes 23048 | tf_op jit(solution)/shard_map/ppermute | solution.py:16
  254.6 9.1 %collective-permute-start.40 = (f32[5,3,4,256]{3,0,2,1:T(8,128)}, f32[5,3,4,256]{3,0,2,1:T(8,128)}, u32[]{:S(2)}, u32[]{:S(2)}) collective-permute-start(f32[5,3,4,256]{3,0,2,1:T(8,128)} %get-tuple-element.15), channel_id=1, source_target_pairs={{1,0},{2,1},{3,2},{4,3},{5,4},{6,5},{7,6},{8,7},{9,8},{10,9},{11,1... | collective-permute-start | bytes 184328 | tf_op jit(solution)/shard_map/ppermute | solution.py:29
  256.5 10.5 %collective-permute-start.41 = (f32[5,3,4,256]{3,0,2,1:T(8,128)}, f32[5,3,4,256]{3,0,2,1:T(8,128)}, u32[]{:S(2)}, u32[]{:S(2)}) collective-permute-start(f32[5,3,4,256]{3,0,2,1:T(8,128)} %get-tuple-element.16), channel_id=1, source_target_pairs={{0,1},{1,2},{2,3},{3,4},{4,5},{5,6},{6,7},{7,8},{8,9},{9,10},{10,1... | collective-permute-start | bytes 184328 | tf_op jit(solution)/shard_map/ppermute | solution.py:27
  273.6 2.1 collective-permute-start.52
  275.7 3.9 %collective-permute-start.53 = (f32[5,384]{1,0:T(8,128)S(1)}, f32[5,384]{1,0:T(8,128)S(1)}, u32[]{:S(2)}, u32[]{:S(2)}) collective-permute-start(f32[5,384]{1,0:T(8,128)S(1)} %collective-permute-done.52), channel_id=1, source_target_pairs={{0,2},{1,3},{2,0},{3,1},{4,6},{5,7},{6,4},{7,5},{8,10},{9,11},{10,... | collective-permute-start | bytes 23048 | tf_op jit(solution)/shard_map/ppermute | solution.py:16
  279.6 5.2 %collective-permute-start.54 = (f32[5,384]{1,0:T(8,128)S(1)}, f32[5,384]{1,0:T(8,128)S(1)}, u32[]{:S(2)}, u32[]{:S(2)}) collective-permute-start(f32[5,384]{1,0:T(8,128)S(1)} %collective-permute-done.53), channel_id=1, source_target_pairs={{0,4},{1,5},{2,6},{3,7},{4,0},{5,1},{6,2},{7,3},{8,12},{9,13},{10,... | collective-permute-start | bytes 23048 | tf_op jit(solution)/shard_map/ppermute | solution.py:16
  284.8 3.7 %collective-permute-start.55 = (f32[5,384]{1,0:T(8,128)S(1)}, f32[5,384]{1,0:T(8,128)S(1)}, u32[]{:S(2)}, u32[]{:S(2)}) collective-permute-start(f32[5,384]{1,0:T(8,128)S(1)} %collective-permute-done.54), channel_id=1, source_target_pairs={{0,8},{1,9},{2,10},{3,11},{4,12},{5,13},{6,14},{7,15},{8,0},{9,1},... | collective-permute-start | bytes 23048 | tf_op jit(solution)/shard_map/ppermute | solution.py:16
  288.5 4.7 %collective-permute-start.56 = (f32[5,384]{1,0:T(8,128)S(1)}, f32[5,384]{1,0:T(8,128)}, u32[]{:S(2)}, u32[]{:S(2)}) collective-permute-start(f32[5,384]{1,0:T(8,128)S(1)} %collective-permute-done.55), channel_id=1, source_target_pairs={{0,16},{1,17},{2,18},{3,19},{4,20},{5,21},{6,22},{7,23},{8,24},{9,... | collective-permute-start | bytes 23048 | tf_op jit(solution)/shard_map/ppermute | solution.py:16
  293.2 7.8 %collective-permute-start.57 = (f32[5,384]{1,0:T(8,128)}, f32[5,384]{1,0:T(8,128)S(1)}, u32[]{:S(2)}, u32[]{:S(2)}) collective-permute-start(f32[5,384]{1,0:T(8,128)} %collective-permute-done.56), channel_id=1, source_target_pairs={{0,32},{1,33},{2,34},{3,35},{4,36},{5,37},{6,38},{7,39},{8,40},{9,... | collective-permute-start | bytes 23048 | tf_op jit(solution)/shard_map/ppermute | solution.py:16
  301.0 3.7 %collective-permute-start.58 = (f32[5,384]{1,0:T(8,128)S(1)}, f32[5,384]{1,0:T(8,128)S(1)}, u32[]{:S(2)}, u32[]{:S(2)}) collective-permute-start(f32[5,384]{1,0:T(8,128)S(1)} %collective-permute-done.57), channel_id=1, source_target_pairs={{0,64},{1,65},{2,66},{3,67},{4,68},{5,69},{6,70},{7,71},{8,72},{9,... | collective-permute-start | bytes 23048 | tf_op jit(solution)/shard_map/ppermute | solution.py:16
  304.7 8.1 %collective-permute-start.59 = (f32[5,384]{1,0:T(8,128)S(1)}, f32[5,384]{1,0:T(8,128)S(1)}, u32[]{:S(2)}, u32[]{:S(2)}) collective-permute-start(f32[5,384]{1,0:T(8,128)S(1)} %collective-permute-done.58), channel_id=1, source_target_pairs={{0,128},{1,129},{2,130},{3,131},{4,132},{5,133},{6,134},{7,135},{8... | collective-permute-start | bytes 23048 | tf_op jit(solution)/shard_map/ppermute | solution.py:16
  308.4 11.1 %collective-permute-start.50 = (f32[5,3,4,256]{3,0,2,1:T(8,128)}, f32[5,3,4,256]{3,0,2,1:T(8,128)}, u32[]{:S(2)}, u32[]{:S(2)}) collective-permute-start(f32[5,3,4,256]{3,0,2,1:T(8,128)} %get-tuple-element.9), channel_id=1, source_target_pairs={{1,0},{2,1},{3,2},{4,3},{5,4},{6,5},{7,6},{8,7},{9,8},{10,9},{11,1... | collective-permute-start | bytes 184328 | tf_op jit(solution)/shard_map/ppermute | solution.py:29
  310.4 10.5 %collective-permute-start.51 = (f32[5,3,4,256]{3,0,2,1:T(8,128)}, f32[5,3,4,256]{3,0,2,1:T(8,128)}, u32[]{:S(2)}, u32[]{:S(2)}) collective-permute-start(f32[5,3,4,256]{3,0,2,1:T(8,128)} %get-tuple-element.10), channel_id=1, source_target_pairs={{0,1},{1,2},{2,3},{3,4},{4,5},{5,6},{6,7},{7,8},{8,9},{9,10},{10,1... | collective-permute-start | bytes 184328 | tf_op jit(solution)/shard_map/ppermute | solution.py:27
  (52 other events, 183.8 us)
where the time goes:
time: 334 us; the launch traced here: 328 us
  waiting for transfers between devices  154 us (46%)
  starting transfers between devices  62.6 us (19%)
  local copies, waits for them, and re-layouts  55.6 us (17%)
  matrix products  33.3 us (10%)
  other arithmetic  20.7 us (6%)
    ppermute x48, waiting for transfers between devices, partner_2(): return lax.ppermute(value, axis, pairs)  142 us
    dot_general x18, matrix products, couple(): jnp.einsum('cd,dikj->cikj', matrix, values, precision=lax.Precision.HIGHEST)  33.3 us
    ppermute x48, starting transfers between devices, partner_2(): return lax.ppermute(value, axis, pairs)  28.6 us
    ppermute x6, starting transfers between devices, extended(): lax.ppermute(head, axis, [((i + 1) % count, i) for i in range(ends)])  19.5 us
    ppermute x6, starting transfers between devices, extended(): lax.ppermute(tail, axis, [(i, (i + 1) % count) for i in range(ends)])  14.4 us
    ppermute x6, waiting for transfers between devices, extended(): lax.ppermute(tail, axis, [(i, (i + 1) % count) for i in range(ends)])  12.1 us
    add x6, other arithmetic, central(): 45.0 * (shifted(1) - shifted(-1)) - 9.0 * (shifted(2) - shifted(-2))  11.8 us
    slice x12, local copies, waits for them, and re-layouts, linear_rhs(): jnp.roll(values, 1, axis=2)  11.5 us
  transfers between devices with their start and end apart: 60, of which 44 were waited for; matrix products, arithmetic and copies ran while one was open for 20% of the time, Pallas kernels for 0%

commit v1 on v0

v1 whole, which is shorter than its diff:
```python
import functools

import jax
import jax.numpy as jnp
from jax import lax
from jax.experimental import pallas as pl
from jax.experimental.pallas import tpu as pltpu
from jax.sharding import PartitionSpec as P

STEPS = 2
time_step = 0.2

FIELDS = 5
REACH = 9
HALO = REACH * STEPS
LANES = 256
STRIP = 32
PLANES = 4
SEGMENTS = 8

f32 = jnp.float32
bf16 = jnp.bfloat16


def iota(shape, axis):
    return lax.broadcasted_iota(jnp.int32, shape, axis)


def lane_index(shape, axis, rows):
    n = iota(shape, axis)
    own = rows * FIELDS
    h = n - own
    comp = jnp.where(n < own, n // rows, h // HALO)
    slot = jnp.where(n < own, HALO + n % rows, h % HALO)
    valid = n < own + FIELDS * HALO
    return jnp.where(valid, comp, -1), jnp.where(valid, slot, -100), n < own


def split(x):
    hi = x.astype(bf16)
    lo = (x - hi.astype(f32)).astype(bf16)
    return hi, lo


def place(values, where_from):
    return jnp.dot(values.astype(bf16), where_from.astype(bf16), preferred_element_type=f32)


def head_or_tail(is_odd, block, first):
    rows = block.shape[0]
    tail, head = block[rows - HALO:], block[:HALO]
    return jnp.where(is_odd == first, head, tail)


def wall_strips(load, count):
    lane = iota((1, 128), 1)
    out = load(0)
    for q in range(1, count):
        out = jnp.where(lane >= q * STRIP, pltpu.roll(load(q), q * STRIP, axis=1), out)
    return out


def pack_kernel(rows, me_ref, pert, ax, ae, sp, blow, mirror_out, even_out, odd_out):
    is_odd = me_ref[0] % 2
    coefs = (ax, ae, sp)
    own = rows * FIELDS
    total = own + rows
    pieces = [
        wall_strips(lambda k, c=c: pert[c, :, k, 0:128], PLANES) for c in range(FIELDS)
    ]
    pieces.append(wall_strips(lambda q: coefs[q][:, 0:128], 3))
    block = jnp.concatenate(pieces, axis=0)
    ri, ci = iota((total, total), 0), iota((total, total), 1)
    turn = ((ri // rows == ci // rows) & (ri % rows == rows - 1 - ci % rows)).astype(f32)
    mirror_out[0:total] = jnp.dot(
        turn, block, precision=lax.Precision.HIGHEST, preferred_element_type=f32
    )
    flags = jnp.broadcast_to(blow[...].astype(f32), (8, rows))
    a, b = iota((rows, 128), 0), iota((rows, 128), 1)
    mirror_out[total:total + 8] = place(flags, b == 2 * rows + rows - 1 - a)
    a, b = iota((rows, LANES), 0), iota((rows, LANES), 1)
    for out, first in ((even_out, 1), (odd_out, 0)):
        for k in range(PLANES):
            for c in range(FIELDS):
                out[k * 96 + c * HALO:k * 96 + (c + 1) * HALO] = head_or_tail(
                    is_odd, pert[c, :, k, :], first
                )
            out[k * 96 + 90:k * 96 + 96] = jnp.zeros((6, LANES), f32)
        for q in range(3):
            out[384 + q * 24:384 + q * 24 + HALO] = head_or_tail(is_odd, coefs[q][...], first)
            out[384 + q * 24 + HALO:384 + q * 24 + 24] = jnp.zeros((24 - HALO, LANES), f32)
        start = jnp.where(is_odd == first, 0, rows - HALO)
        base = own + 2 * HALO
        out[456:464] = place(flags, (b - base == a - start) & (b >= base) & (b < base + HALO))


def pack_strips_kernel(rows, me_ref, strips, even_out, odd_out):
    is_odd = me_ref[0] % 2
    own = rows * FIELDS
    b, a = iota((128, 128), 1), iota((128, 128), 0)
    for out, first in ((even_out, 1), (odd_out, 0)):
        for c in range(FIELDS):
            out[c * HALO:(c + 1) * HALO] = head_or_tail(
                is_odd, strips[c * rows:(c + 1) * rows], first
            )
        out[90:96] = jnp.zeros((6, 128), f32)
        out[96:96 + HALO] = head_or_tail(is_odd, strips[own:own + rows], first)
        out[96 + HALO:120] = jnp.zeros((24 - HALO, 128), f32)
        start = jnp.where(is_odd == first, 0, rows - HALO)
        base = own + 2 * HALO - 128
        out[120:128] = place(
            strips[own + rows:own + rows + 8],
            (b - base == a - 2 * rows - start) & (b >= base) & (b < base + HALO),
        )


def main_kernel(
    rows, total_rows, me_ref, cut_ref, cxi, ceta, cspan,
    pert, ax, ae, sp, blow, strips, even_in, odd_in, even_strips, odd_strips,
    out,
    vnat, xs, v0, xe, gs, gv, ge, rr, zz, coef, coef_e, gcoef, gcoef_e, lanes_ref,
    w1, w2, wm, wbase, ynat,
):
    me = me_ref[0]
    is_odd = me % 2
    own = rows * FIELDS
    slots = rows + HALO
    coefs_in = (ax, ae, sp)
    scales = (-time_step / 60.0, -time_step / 60.0, -time_step)
    last = pl.num_programs

    rc, rs, _ = lane_index((LANES, LANES), 0, rows)
    cc, cs, _ = lane_index((LANES, LANES), 1, rows)
    apart = jnp.where((rs >= 0) & (cs >= 0), (rs - cs + slots) % slots, 0)
    band = jnp.zeros((LANES, LANES), f32)
    for d, value in ((1, 45.0), (2, -9.0), (3, 1.0)):
        band = jnp.where(apart == d, value, band)
        band = jnp.where(apart == slots - d, -value, band)
    same = ((rs == cs) & (rs >= 0)).astype(f32)
    col_comp, _, _ = lane_index((1, LANES), 1, rows)

    def spread(matrix):
        total = jnp.zeros((LANES, LANES), f32)
        for d in range(FIELDS):
            line = jnp.zeros((1, LANES), f32)
            for c in range(FIELDS):
                line = jnp.where(col_comp == c, matrix[c, d], line)
            total = jnp.where(rc == d, line, total)
        return total

    hi, lo = split(spread(cxi) * band * (-time_step / 60.0))
    wbase[0:LANES] = hi
    wbase[LANES:2 * LANES] = lo
    wbase[2 * LANES:3 * LANES] = jnp.where(rc == cc, band, 0.0).astype(bf16)
    hi, lo = split(spread(ceta) * same * (-time_step / 60.0))
    w1[3 * LANES:4 * LANES] = hi
    w1[4 * LANES:5 * LANES] = lo
    w1[5 * LANES:6 * LANES] = hi
    hi, lo = split(spread(cspan) * same * (-time_step * 0.5))
    w2[0:LANES] = hi
    w2[LANES:2 * LANES] = lo
    w2[2 * LANES:3 * LANES] = hi

    def set_xi_weights(low, high):
        keep = jnp.where((rs >= low) & (rs < high), 0.0, 1.0).astype(bf16)
        hi, lo = wbase[0:LANES] * keep, wbase[LANES:2 * LANES] * keep
        w1[0:LANES] = hi
        w1[LANES:2 * LANES] = lo
        w1[2 * LANES:3 * LANES] = hi
        m = wbase[2 * LANES:3 * LANES] * keep
        wm[0:LANES] = m
        wm[LANES:2 * LANES] = m

    comp, slot, is_own = lane_index((1, LANES), 1, rows)
    sign = jnp.where(comp == 2, -1.0, 1.0).astype(f32)
    a, b = iota((rows, LANES), 0), iota((rows, LANES), 1)
    own_flags = place(
        jnp.broadcast_to(blow[...].astype(f32), (8, rows)), b == 2 * rows + a
    )
    own_mirror = jnp.concatenate(
        [strips[own + rows:own + rows + 8], jnp.zeros((8, LANES - 128), f32)], axis=1
    )

    def cut_lanes(g):
        i = me * rows + g - HALO
        mirror = total_rows - 1 - i
        inside = ((i >= cut_ref[0]) & (i < cut_ref[1])) | (
            (mirror >= cut_ref[0]) & (mirror < cut_ref[1])
        )
        return inside.astype(f32)

    def to_segments(natural, store):
        ynat[0] = natural[:, 0:128].T
        ynat[1] = natural[:, 128:256].T
        return ynat

    def transposed(block):
        return block.T

    def read_window(halo, halo_strips, halo_right):
        for k in range(PLANES):
            for c in range(FIELDS):
                vnat[c * rows:(c + 1) * rows] = pert[c, :, k, :]
            vnat[own:LANES] = halo[k * 96:(k + 1) * 96]
            for t in range(2):
                ynat[t] = vnat[t * 128:(t + 1) * 128].T
            for jl in range(32):
                for t in range(2):
                    xs[k, 3 + jl, :, t * 128:(t + 1) * 128] = ynat[
                        t, pl.ds(jl, SEGMENTS, stride=32), :
                    ]
        for q in range(3):
            for c in range(FIELDS):
                vnat[c * rows:(c + 1) * rows] = coefs_in[q][...]
                vnat[own + c * HALO:own + (c + 1) * HALO] = halo[
                    384 + q * 24:384 + q * 24 + HALO
                ]
            vnat[own + FIELDS * HALO:LANES] = jnp.zeros((LANES - own - FIELDS * HALO, LANES), f32)
            for t in range(2):
                ynat[t] = vnat[t * 128:(t + 1) * 128].T * scales[q]
            for jl in range(32):
                for t in range(2):
                    coef[q, jl, :, t * 128:(t + 1) * 128] = ynat[
                        t, pl.ds(jl, SEGMENTS, stride=32), :
                    ]
        vnat[0:own, 0:128] = strips[0:own]
        vnat[own:LANES, 0:128] = halo_strips[0:96]
        for t in range(2):
            ynat[t, 0:128] = vnat[t * 128:(t + 1) * 128, 0:128].T
        for m in range(HALO):
            for t in range(2):
                line = ynat[t, pl.ds(m, PLANES, stride=STRIP), :]
                gs[3 + m, 0:4, t * 128:(t + 1) * 128] = line
                gs[3 + m, 4:8, t * 128:(t + 1) * 128] = line
        for c in range(FIELDS):
            vnat[c * rows:(c + 1) * rows, 0:128] = strips[own:own + rows]
            vnat[own + c * HALO:own + (c + 1) * HALO, 0:128] = halo_strips[96:96 + HALO]
        for t in range(2):
            ynat[t, 0:128] = vnat[t * 128:(t + 1) * 128, 0:128].T
        for q in range(3):
            for m in range(HALO):
                for t in range(2):
                    gcoef[q, m, :, t * 128:(t + 1) * 128] = jnp.broadcast_to(
                        ynat[t, q * STRIP + m:q * STRIP + m + 1, :] * scales[q], (8, 128)
                    )
        g = jnp.where(is_own, slot, jnp.where(halo_right == 1, slots + slot, slot))
        lanes_ref[0] = jnp.broadcast_to(cut_lanes(g), (8, LANES))
        lanes_ref[1] = 2.0 * (own_flags + halo[456:464])
        lanes_ref[2] = 2.0 * (
            own_mirror
            + jnp.concatenate([jnp.zeros((8, 128), f32), halo_strips[120:128]], axis=1)
        )

    sub = iota((8, LANES), 0)

    def pressure(line):
        near = pltpu.roll(line, LANES - 2 * rows, axis=1)
        far = pltpu.roll(line, LANES - 2 * HALO, axis=1)
        return jnp.where(is_own, near, far)

    def slopes(load, offset):
        return (
            45.0 * (load(offset + 1) - load(offset - 1))
            - 9.0 * (load(offset + 2) - load(offset - 2))
            + (load(offset + 3) - load(offset - 3))
        )

    def time_stage(depth, alpha, beta):
        cut = lanes_ref[0] > 0.5
        wall = []
        for m in range(3):
            line = jnp.concatenate([xs[k, 3 + m, 0:1, :] for k in range(PLANES)], axis=0)
            wall.append(jnp.concatenate([line, line], axis=0))
        wall_g = [gs[3 + m] for m in range(3)]
        lift = lanes_ref[1] * jnp.where(comp == 2, pressure(wall[0]), 0.0)
        lift_g = lanes_ref[2] * jnp.where(comp == 2, pressure(wall_g[0]), 0.0)
        for m in range(3):
            ghost = jnp.where(cut, sign * wall_g[m], sign * wall[m] + lift)
            gs[2 - m] = jnp.where(cut, sign * wall[m], sign * wall_g[m] + lift_g)
            for k in range(PLANES):
                below = pltpu.roll(xs[k, 34 - m], 1, axis=0)
                xs[k, 2 - m] = jnp.where(sub == 0, ghost[k:k + 1], below)
                above = pltpu.roll(xs[k, 3 + m], SEGMENTS - 1, axis=0)
                xs[k, 35 + m] = jnp.where(sub == SEGMENTS - 1, 0.0, above)
        for k in range(PLANES):
            x = xs[k, 3:35].reshape(LANES, LANES)
            e = slopes(lambda at: xs[k, at:at + 32], 3).reshape(LANES, LANES)
            xh, xl = split(x)
            eh, el = split(e)
            first = jnp.dot(
                jnp.concatenate([xh, xh, xl, eh, eh, el], axis=1), w1[...],
                preferred_element_type=f32,
            )
            grad = jnp.dot(
                jnp.concatenate([xh, xl], axis=1), wm[...], preferred_element_type=f32
            )
            zz[k] = jnp.dot(
                jnp.concatenate([xh, xh, xl], axis=1), w2[...], preferred_element_type=f32
            )
            ca = coef[0].reshape(LANES, LANES)
            cb = coef[1].reshape(LANES, LANES)
            cd = coef[2].reshape(LANES, LANES)
            rr[k] = first + ca * grad + cb * e + cd * x
        n = depth * 8
        x = gs[3:3 + depth].reshape(n, LANES)
        e = slopes(lambda at: gs[at:at + depth], 3).reshape(n, LANES)
        xh, xl = split(x)
        eh, el = split(e)
        first = jnp.dot(
            jnp.concatenate([-xh, -xh, -xl, eh, eh, el], axis=1), w1[...],
            preferred_element_type=f32,
        )
        grad = jnp.dot(
            jnp.concatenate([-xh, -xl], axis=1), wm[...], preferred_element_type=f32
        )
        z = jnp.dot(
            jnp.concatenate([xh, xh, xl], axis=1), w2[...], preferred_element_type=f32
        ).reshape(depth, 8, LANES)
        span = pltpu.roll(z, 7, axis=1) - pltpu.roll(z, 1, axis=1)
        ca, cb, cd = (gcoef[q, 0:depth].reshape(n, LANES) for q in range(3))
        r = (first + ca * grad + cb * e + cd * x).reshape(depth, 8, LANES) + span
        gs[3:3 + depth] = alpha * gv[0:depth] + beta * (gs[3:3 + depth] + r)
        for k in range(PLANES):
            r = rr[k] + (zz[(k + 1) % PLANES] - zz[(k - 1) % PLANES])
            x = xs[k, 3:35] + r.reshape(32, 8, LANES)
            xs[k, 3:35] = alpha * v0[k] + beta * x

    def time_steps(depth):
        for k in range(PLANES):
            v0[k] = xs[k, 3:35]
        gv[0:depth] = gs[3:3 + depth]

        def stage(s, carry):
            alpha = jnp.where(s == 0, 0.0, jnp.where(s == 1, 0.75, 1.0 / 3.0)).astype(f32)
            beta = jnp.where(s == 0, 1.0, jnp.where(s == 1, 0.25, 2.0 / 3.0)).astype(f32)
            time_stage(depth, alpha, beta)
            return carry

        lax.fori_loop(0, 3, stage, 0)

    at_start = me == 0
    at_end = me == total_rows // rows - 1
    gs[...] = jnp.zeros(gs.shape, f32)
    set_xi_weights(0, 0)
    read_window(even_in, even_strips, 1 - is_odd)
    time_steps(HALO - 3)
    for k in range(PLANES):
        xe[k] = xs[k, 3:35]
    ge[...] = gs[3:3 + REACH]
    coef_e[...] = coef[...]
    gcoef_e[...] = gcoef[:, 0:REACH]
    blow_e, blow_ge = lanes_ref[1], lanes_ref[2]
    outside = at_start | at_end
    set_xi_weights(0, jnp.where(outside, HALO, 0))
    read_window(odd_in, odd_strips, is_odd)
    time_steps(HALO - 3)
    set_xi_weights(
        jnp.where(at_start, REACH, 0),
        jnp.where(at_start, HALO, jnp.where(at_end, REACH, 0)),
    )
    left = (slot >= REACH) & (slot < REACH + rows)
    from_e = jnp.where(left, is_odd, 1 - is_odd) == 1
    for k in range(PLANES):
        xs[k, 3:35] = jnp.where(from_e, xe[k], xs[k, 3:35])
    gs[3:3 + REACH] = jnp.where(from_e, ge[...], gs[3:3 + REACH])
    coef[...] = jnp.where(from_e, coef_e[...], coef[...])
    gcoef[:, 0:REACH] = jnp.where(from_e, gcoef_e[...], gcoef[:, 0:REACH])
    g = jnp.where(is_own, slot, jnp.where(slot < REACH, slots + slot, slot))
    lanes_ref[0] = jnp.broadcast_to(cut_lanes(g), (8, LANES))
    lanes_ref[1] = jnp.where(from_e, blow_e, lanes_ref[1])
    lanes_ref[2] = jnp.where(from_e, blow_ge, lanes_ref[2])
    time_steps(REACH - 3)
    for k in range(PLANES):
        for jl in range(32):
            for t in range(2):
                ynat[t, pl.ds(jl, SEGMENTS, stride=32), :] = xs[
                    k, 3 + jl, :, t * 128:(t + 1) * 128
                ]
        low, high = ynat[0].T, ynat[1].T
        for c in range(FIELDS):
            at = c * rows
            out[c, :, k, :] = low[at:at + rows] if at < 128 else high[at - 128:at - 128 + rows]


def on_device(
    perturbation, advect_xi, advect_eta, sponge,
    couple_xi, couple_eta, couple_span, wake_cut, blowing,
):
    rows = perturbation.shape[1]
    devices = lax.axis_size("wrap")
    total_rows = rows * devices
    own = rows * FIELDS
    me = lax.axis_index("wrap").astype(jnp.int32).reshape(1)
    flags = blowing.reshape(1, rows)
    mirror = [(i, devices - 1 - i) for i in range(devices)]
    same_chip = [(i, i ^ 1) for i in range(devices)]
    next_chip = [(i, i + 1 if i % 2 else i - 1) for i in range(1, devices - 1)]

    vmem = pl.BlockSpec(memory_space=pltpu.VMEM)
    smem = pl.BlockSpec(memory_space=pltpu.SMEM)
    params = pltpu.CompilerParams(vmem_limit_bytes=48 * 1024 * 1024)

    def shape(*dims):
        return jax.ShapeDtypeStruct(dims, f32)

    to_mirror, to_same, to_next = pl.pallas_call(
        functools.partial(pack_kernel, rows),
        out_shape=(shape(own + rows + 8, 128), shape(464, LANES), shape(464, LANES)),
        in_specs=[smem] + [vmem] * 5,
        out_specs=(vmem,) * 3,
        compiler_params=params,
    )(me, perturbation, advect_xi, advect_eta, sponge, flags)

    strips = lax.ppermute(to_mirror, "wrap", mirror)
    from_same = lax.ppermute(to_same, "wrap", same_chip)
    from_next = lax.ppermute(to_next, "wrap", next_chip)

    strip_same, strip_next = pl.pallas_call(
        functools.partial(pack_strips_kernel, rows),
        out_shape=(shape(128, 128), shape(128, 128)),
        in_specs=[smem, vmem],
        out_specs=(vmem,) * 2,
        compiler_params=params,
    )(me, strips)
    strips_same = lax.ppermute(strip_same, "wrap", same_chip)
    strips_next = lax.ppermute(strip_next, "wrap", next_chip)

    state = (PLANES, 32, SEGMENTS, LANES)
    scratch = [
        pltpu.VMEM((LANES, LANES), f32),
        pltpu.VMEM((PLANES, 38, SEGMENTS, LANES), f32),
        pltpu.VMEM(state, f32),
        pltpu.VMEM(state, f32),
        pltpu.VMEM((3 + HALO + 3, 8, LANES), f32),
        pltpu.VMEM((HALO, 8, LANES), f32),
        pltpu.VMEM((REACH, 8, LANES), f32),
        pltpu.VMEM((PLANES, LANES, LANES), f32),
        pltpu.VMEM((PLANES, LANES, LANES), f32),
        pltpu.VMEM((3, 32, SEGMENTS, LANES), f32),
        pltpu.VMEM((3, 32, SEGMENTS, LANES), f32),
        pltpu.VMEM((3, HALO, 8, LANES), f32),
        pltpu.VMEM((3, REACH, 8, LANES), f32),
        pltpu.VMEM((3, 8, LANES), f32),
        pltpu.VMEM((6 * LANES, LANES), bf16),
        pltpu.VMEM((3 * LANES, LANES), bf16),
        pltpu.VMEM((2 * LANES, LANES), bf16),
        pltpu.VMEM((3 * LANES, LANES), bf16),
        pltpu.VMEM((2, LANES, 128), f32),
    ]
    return pl.pallas_call(
        functools.partial(main_kernel, rows, total_rows),
        out_shape=shape(*perturbation.shape),
        in_specs=[smem] * 5 + [vmem] * 10,
        out_specs=vmem,
        scratch_shapes=scratch,
        compiler_params=params,
    )(
        me, wake_cut, couple_xi, couple_eta, couple_span,
        perturbation, advect_xi, advect_eta, sponge, flags,
        strips, from_same, from_next, strips_same, strips_next,
    )


def solution(mesh):
    in_specs = (
        P(None, "wrap", None, None),
        P("wrap", None),
        P("wrap", None),
        P("wrap", None),
        P(),
        P(),
        P(),
        P(),
        P("wrap"),
    )
    out_specs = P(None, "wrap", None, None)
    return jax.shard_map(
        on_device, mesh=mesh, in_specs=in_specs, out_specs=out_specs, check_vma=False
    )
```

time: 334 us -> 65.2 us (0.20); the launches traced: 328 us -> 64.8 us
  waiting for transfers between devices: 154 us -> 12.5 us
  local copies, waits for them, and re-layouts: 55.6 us -> 4.03 us
  starting transfers between devices: 62.6 us -> 20.1 us
  matrix products: 33.3 us -> 0 us
  Pallas kernels: 0 us -> 28.1 us
  other arithmetic: 20.7 us -> 0 us
    ppermute x60 -> x5, waiting for transfers between devices: 154 us -> 12.5 us  [the longest x1 10.6 us: on_device(): strips = lax.ppermute(to_mirror, 'wrap', mirror)]
    ppermute x60 -> x5, starting transfers between devices: 62.6 us -> 20.1 us  [the longest x1 10.3 us: on_device(): from_next = lax.ppermute(to_next, 'wrap', next_chip)]
    dot_general x18 -> x0, matrix products: 33.3 us -> none  [couple(): jnp.einsum('cd,dikj->cikj', matrix, values, precision=lax.Precision.HIGHEST)]
    pallas_call x0 -> x3, Pallas kernels: none -> 28.1 us  [the longest x1 27.1 us: on_device(): pl.pallas_call(functools.partial(main_kernel, rows, total_rows), out_shap...]
    slice x55 -> x0, local copies, waits for them, and re-layouts: 19.1 us -> none  [the longest x12 11.5 us: linear_rhs(): jnp.roll(values, 1, axis=2)]
    reshape x18 -> x0, local copies, waits for them, and re-layouts: 14.2 us -> none  [the longest x12 10.3 us: partner(): return arrived.reshape(wall_strip.shape)[:, ::-1]]
    add x12 -> x0, other arithmetic: 11.8 us -> none  [the longest x6 11.8 us: central(): 45.0 * (shifted(1) - shifted(-1)) - 9.0 * (shifted(2) - shifted(-2))]
    rev x12 -> x0, local copies, waits for them, and re-layouts: 7.12 us -> none  [the longest x6 5.17 us: wall_ghost(): mirrored = mirror_strip[:, :, :, ::-1] * flip_sign()]
  transfers between devices with their start and end apart: 60 -> 5, of which waited for: 44 -> 2; matrix products, arithmetic and copies ran while one was open for 20% -> 0% of each run, Pallas kernels for 0% -> 0%
where the time goes in v1:
time: 65.2 us; the launch traced here: 64.8 us
  Pallas kernels  28.1 us (43%)
  starting transfers between devices  20.1 us (31%)
  waiting for transfers between devices  12.5 us (19%)
  local copies, waits for them, and re-layouts  4.03 us (6%)
    pallas_call x1, Pallas kernels, on_device(): pl.pallas_call(functools.partial(main_kernel, rows, total_rows), out_shap...  27.1 us
    ppermute x1, waiting for transfers between devices, on_device(): strips = lax.ppermute(to_mirror, 'wrap', mirror)  10.6 us
    ppermute x1, starting transfers between devices, on_device(): from_next = lax.ppermute(to_next, 'wrap', next_chip)  10.3 us
    ppermute x1, starting transfers between devices, on_device(): strips_next = lax.ppermute(strip_next, 'wrap', next_chip)  8.64 us
    unnamed x20, local copies, waits for them, and re-layouts  4.03 us
    ppermute x1, waiting for transfers between devices, on_device(): strips_next = lax.ppermute(strip_next, 'wrap', next_chip)  1.92 us
  transfers between devices with their start and end apart: 5, of which 2 were waited for; matrix products, arithmetic and copies ran while one was open for 0% of the time, Pallas kernels for 0%

profile of v1, /device:TPU:2, one launch (start us, length us, event | category | flops | bytes accessed | tf_op | source)
XLA Modules:
  0.0 64.8 jit_solution(17568087578883621128)
XLA Ops:
  0.0 0.0 copy-start.8
  0.0 0.7 %copy-done.8 = s32[32]{0:T(128)S(1)} copy-done((s32[32]{0:T(128)S(1)}, s32[32]{0:T(128)}, u32[]{:S(2)}) %copy-start.8) | copy-done | bytes 152
  0.7 0.0 copy-start
  0.7 1.1 %copy-done = f32[5,32,4,256]{3,2,1,0:T(4,128)S(1)} copy-done((f32[5,32,4,256]{3,2,1,0:T(4,128)S(1)}, f32[5,32,4,256]{3,2,1,0:T(4,128)}, u32[]{:S(2)}) %copy-start) | copy-done | bytes 655384
  1.7 0.0 copy-start.2
  1.7 0.8 %copy-done.2 = f32[32,256]{1,0:T(8,128)S(1)} copy-done((f32[32,256]{1,0:T(8,128)S(1)}, f32[32,256]{1,0:T(8,128)}, u32[]{:S(2)}) %copy-start.2) | copy-done | bytes 32792
  2.5 0.0 copy-start.3
  2.5 0.8 %copy-done.3 = f32[32,256]{1,0:T(8,128)S(1)} copy-done((f32[32,256]{1,0:T(8,128)S(1)}, f32[32,256]{1,0:T(8,128)}, u32[]{:S(2)}) %copy-start.3) | copy-done | bytes 32792
  3.3 0.0 copy-start.4
  3.3 0.8 %copy-done.4 = f32[32,256]{1,0:T(8,128)S(1)} copy-done((f32[32,256]{1,0:T(8,128)S(1)}, f32[32,256]{1,0:T(8,128)}, u32[]{:S(2)}) %copy-start.4) | copy-done | bytes 32792
  4.0 0.0 copy-start.1
  4.0 0.9 %shard_map.91 = (f32[200,128]{1,0:T(8,128)S(1)}, f32[464,256]{1,0:T(8,128)S(1)}, f32[464,256]{1,0:T(8,128)S(1)}) custom-call(s32[1]{0:T(128)} %bitcast.me_ref, f32[5,32,4,256]{3,2,1,0:T(4,128)S(1)} %copy-done, f32[32,256]{1,0:T(8,128)S(1)} %copy-done.2, f32[32,256]{1,0:T(8,128)S(1)} %copy-done.3, f32[32,256]{1,0:T(8,128)S(1)} %copy-done.4, s32[1,32]{1,0:T(1,128)S(1)} %bitcast.2), custom_call_target="tpu_custom_call" | custom-call | tf_op jit(solution)/shard_map/pallas_call | solution.py:406
  4.9 0.1 collective-permute-start.1
  5.0 10.3 %collective-permute-start.2 = (f32[464,256]{1,0:T(8,128)S(1)}, f32[464,256]{1,0:T(8,128)S(1)}, u32[]{:S(2)}, u32[]{:S(2)}) collective-permute-start(f32[464,256]{1,0:T(8,128)S(1)} %get-tuple-element.12), channel_id=1, source_target_pairs={{1,2},{2,1},{3,4},{4,3},{5,6},{6,5},{7,8},{8,7},{9,10},{10,9},{11,... | collective-permute-start | bytes 1425416 | tf_op jit(solution)/shard_map/ppermute | solution.py:416
  15.3 1.1 %collective-permute-start = (f32[200,128]{1,0:T(8,128)S(1)}, f32[200,128]{1,0:T(8,128)S(1)}, u32[]{:S(2)}, u32[]{:S(2)}) collective-permute-start(f32[200,128]{1,0:T(8,128)S(1)} %get-tuple-element.10), channel_id=1, source_target_pairs={{0,255},{1,254},{2,253},{3,252},{4,251},{5,250},{6,249},{7,248},{8... | collective-permute-start | bytes 307208 | tf_op jit(solution)/shard_map/ppermute | solution.py:414
  16.4 10.6 %collective-permute-done.strips = f32[200,128]{1,0:T(8,128)S(1)} collective-permute-done((f32[200,128]{1,0:T(8,128)S(1)}, f32[200,128]{1,0:T(8,128)S(1)}, u32[]{:S(2)}, u32[]{:S(2)}) %collective-permute-start) | collective-permute-done | bytes 102432 | tf_op jit(solution)/shard_map/ppermute | solution.py:414
  27.0 0.0 copy-start.5
  27.0 0.0 copy-start.6
  27.0 0.0 copy-start.7
  27.0 0.1 shard_map.92
  27.1 0.0 copy-start.9
  27.1 0.0 collective-permute-start.3
  27.1 8.6 %collective-permute-start.4 = (f32[128,128]{1,0:T(8,128)S(1)}, f32[128,128]{1,0:T(8,128)S(1)}, u32[]{:S(2)}, u32[]{:S(2)}) collective-permute-start(f32[128,128]{1,0:T(8,128)S(1)} %get-tuple-element.14), channel_id=1, source_target_pairs={{1,2},{2,1},{3,4},{4,3},{5,6},{6,5},{7,8},{8,7},{9,10},{10,9},{11,... | collective-permute-start | bytes 196616 | tf_op jit(solution)/shard_map/ppermute | solution.py:426
  35.8 0.0 collective-permute-done.3.even_strips
  35.8 1.9 %collective-permute-done.4.odd_strips = f32[128,128]{1,0:T(8,128)S(1)} collective-permute-done((f32[128,128]{1,0:T(8,128)S(1)}, f32[128,128]{1,0:T(8,128)S(1)}, u32[]{:S(2)}, u32[]{:S(2)}) %collective-permute-start.4) | collective-permute-done | bytes 65568 | tf_op jit(solution)/shard_map/ppermute | solution.py:426
  37.7 0.0 collective-permute-done.1.even_in
  37.7 0.0 collective-permute-done.2.odd_in
  37.7 0.0 copy-done.1
  37.7 0.0 copy-done.5
  37.7 0.0 copy-done.6
  37.7 0.0 copy-done.7
  37.8 0.0 copy-done.9
  37.8 27.1 %shard_map.93 = f32[5,32,4,256]{3,2,1,0:T(4,128)} custom-call(s32[1]{0:T(128)} %bitcast.me_ref, s32[2]{0:T(128)S(1)} %copy-done.9, f32[5,5]{1,0:T(8,128)S(1)} %copy-done.5, f32[5,5]{1,0:T(8,128)S(1)} %copy-done.6, f32[5,5]{1,0:T(8,128)S(1)} %copy-done.7, f32[5,32,4,256]{3,2,1,0:T(4,128)S(1)} %copy-done.1, f32[32,256]{1,0:T(8,128)S(1)} %copy-done.2, ...), custom_call_target="tpu_custom_call" | custom-call | tf_op jit(solution)/shard_map/pallas_call | solution.py:450
Async XLA Ops:
  0.0 0.7 %copy-start.8 = (s32[32]{0:T(128)S(1)}, s32[32]{0:T(128)}, u32[]{:S(2)}) copy-start(s32[32]{0:T(128)} %param.17) | copy-start | bytes 388
  0.7 1.1 %copy-start = (f32[5,32,4,256]{3,2,1,0:T(4,128)S(1)}, f32[5,32,4,256]{3,2,1,0:T(4,128)}, u32[]{:S(2)}) copy-start(f32[5,32,4,256]{3,2,1,0:T(4,128)} %pert.3) | copy-start | bytes 1966084
  1.7 0.8 %copy-start.2 = (f32[32,256]{1,0:T(8,128)S(1)}, f32[32,256]{1,0:T(8,128)}, u32[]{:S(2)}) copy-start(f32[32,256]{1,0:T(8,128)} %ax.3) | copy-start | bytes 98308
  2.5 0.8 %copy-start.3 = (f32[32,256]{1,0:T(8,128)S(1)}, f32[32,256]{1,0:T(8,128)}, u32[]{:S(2)}) copy-start(f32[32,256]{1,0:T(8,128)} %ae.3) | copy-start | bytes 98308
  3.3 0.8 %copy-start.4 = (f32[32,256]{1,0:T(8,128)S(1)}, f32[32,256]{1,0:T(8,128)}, u32[]{:S(2)}) copy-start(f32[32,256]{1,0:T(8,128)} %sp.3) | copy-start | bytes 98308
  4.0 33.7 %copy-start.1 = (f32[5,32,4,256]{3,2,1,0:T(4,128)S(1)}, f32[5,32,4,256]{3,2,1,0:T(4,128)}, u32[]{:S(2)}) copy-start(f32[5,32,4,256]{3,2,1,0:T(4,128)} %pert.3) | copy-start | bytes 1966084
  4.9 32.8 %collective-permute-start.1 = (f32[464,256]{1,0:T(8,128)S(1)}, f32[464,256]{1,0:T(8,128)S(1)}, u32[]{:S(2)}, u32[]{:S(2)}) collective-permute-start(f32[464,256]{1,0:T(8,128)S(1)} %get-tuple-element.11), channel_id=1, source_target_pairs={{0,1},{1,0},{2,3},{3,2},{4,5},{5,4},{6,7},{7,6},{8,9},{9,8},{10,11... | collective-permute-start | bytes 1425416 | tf_op jit(solution)/shard_map/ppermute | solution.py:415
  5.0 32.7 %collective-permute-start.2 = (f32[464,256]{1,0:T(8,128)S(1)}, f32[464,256]{1,0:T(8,128)S(1)}, u32[]{:S(2)}, u32[]{:S(2)}) collective-permute-start(f32[464,256]{1,0:T(8,128)S(1)} %get-tuple-element.12), channel_id=1, source_target_pairs={{1,2},{2,1},{3,4},{4,3},{5,6},{6,5},{7,8},{8,7},{9,10},{10,9},{11,... | collective-permute-start | bytes 1425416 | tf_op jit(solution)/shard_map/ppermute | solution.py:416
  15.3 11.7 %collective-permute-start = (f32[200,128]{1,0:T(8,128)S(1)}, f32[200,128]{1,0:T(8,128)S(1)}, u32[]{:S(2)}, u32[]{:S(2)}) collective-permute-start(f32[200,128]{1,0:T(8,128)S(1)} %get-tuple-element.10), channel_id=1, source_target_pairs={{0,255},{1,254},{2,253},{3,252},{4,251},{5,250},{6,249},{7,248},{8... | collective-permute-start | bytes 307208 | tf_op jit(solution)/shard_map/ppermute | solution.py:414
  27.0 10.8 %copy-start.5 = (f32[5,5]{1,0:T(8,128)S(1)}, f32[5,5]{1,0:T(8,128)}, u32[]{:S(2)}) copy-start(f32[5,5]{1,0:T(8,128)} %cxi.1) | copy-start | bytes 304
  27.0 10.8 %copy-start.6 = (f32[5,5]{1,0:T(8,128)S(1)}, f32[5,5]{1,0:T(8,128)}, u32[]{:S(2)}) copy-start(f32[5,5]{1,0:T(8,128)} %ceta.1) | copy-start | bytes 304
  27.0 10.8 %copy-start.7 = (f32[5,5]{1,0:T(8,128)S(1)}, f32[5,5]{1,0:T(8,128)}, u32[]{:S(2)}) copy-start(f32[5,5]{1,0:T(8,128)} %cspan.1) | copy-start | bytes 304
  27.1 10.6 %copy-start.9 = (s32[2]{0:T(128)S(1)}, s32[2]{0:T(128)}, u32[]{:S(2)}) copy-start(s32[2]{0:T(128)} %cut_ref.1) | copy-start | bytes 28
  27.1 8.7 %collective-permute-start.3 = (f32[128,128]{1,0:T(8,128)S(1)}, f32[128,128]{1,0:T(8,128)S(1)}, u32[]{:S(2)}, u32[]{:S(2)}) collective-permute-start(f32[128,128]{1,0:T(8,128)S(1)} %get-tuple-element.13), channel_id=1, source_target_pairs={{0,1},{1,0},{2,3},{3,2},{4,5},{5,4},{6,7},{7,6},{8,9},{9,8},{10,11... | collective-permute-start | bytes 196616 | tf_op jit(solution)/shard_map/ppermute | solution.py:425
  27.1 10.6 %collective-permute-start.4 = (f32[128,128]{1,0:T(8,128)S(1)}, f32[128,128]{1,0:T(8,128)S(1)}, u32[]{:S(2)}, u32[]{:S(2)}) collective-permute-start(f32[128,128]{1,0:T(8,128)S(1)} %get-tuple-element.14), channel_id=1, source_target_pairs={{1,2},{2,1},{3,4},{4,3},{5,6},{6,5},{7,8},{8,7},{9,10},{10,9},{11,... | collective-permute-start | bytes 196616 | tf_op jit(solution)/shard_map/ppermute | solution.py:426

commit v2 on v1

v2 whole, which is shorter than its diff:
```python
import functools

import jax
import jax.numpy as jnp
from jax import lax
from jax.experimental import pallas as pl
from jax.experimental.pallas import tpu as pltpu
from jax.sharding import PartitionSpec as P

STEPS = 2
time_step = 0.2

FIELDS = 5
REACH = 9
HALO = REACH * STEPS
LANES = 256
STRIP = 32
PLANES = 4
SEGMENTS = 8

PAYLOAD = 464
SCALES = (-time_step / 60.0, -time_step * 45.0 / 60.0, -time_step)
KEEPS = (0.0, 0.0, 1.0)

f32 = jnp.float32
bf16 = jnp.bfloat16
f8 = jnp.float8_e5m2

HELD = 16.0


def iota(shape, axis):
    return lax.broadcasted_iota(jnp.int32, shape, axis)


def lane_index(shape, axis, rows):
    n = iota(shape, axis)
    own = rows * FIELDS
    h = n - own
    comp = jnp.where(n < own, n // rows, h // HALO)
    slot = jnp.where(n < own, HALO + n % rows, h % HALO)
    valid = n < own + FIELDS * HALO
    return jnp.where(valid, comp, -1), jnp.where(valid, slot, -100), n < own


def split(x):
    hi = x.astype(bf16)
    lo = (x - hi.astype(f32)).astype(bf16)
    return hi, lo


def split_small(x):
    hi = x.astype(bf16)
    return hi, (x - hi.astype(f32)).astype(f8)


def place(values, where_from):
    return jnp.dot(values.astype(bf16), where_from.astype(bf16), preferred_element_type=f32)


def head_or_tail(is_odd, block, first):
    rows = block.shape[0]
    tail, head = block[rows - HALO:], block[:HALO]
    return jnp.where(is_odd == first, head, tail)


def wall_strips(load, count):
    lane = iota((1, 128), 1)
    out = load(0)
    for q in range(1, count):
        out = jnp.where(lane >= q * STRIP, pltpu.roll(load(q), q * STRIP, axis=1), out)
    return out


def pack_mirror_kernel(
    rows, pert_hbm, ax_hbm, ae_hbm, sp_hbm, blow, mirror_out, pert, coefs, sems
):
    near = pl.ds(0, 128)
    copies = [pltpu.make_async_copy(pert_hbm.at[:, :, :, near], pert, sems.at[0])]
    for q, ref in enumerate((ax_hbm, ae_hbm, sp_hbm)):
        copies.append(pltpu.make_async_copy(ref.at[:, near], coefs.at[q], sems.at[1 + q]))
    for copy in copies:
        copy.start()
    own = rows * FIELDS
    total = own + rows
    ri, ci = iota((total, total), 0), iota((total, total), 1)
    turn = ((ri // rows == ci // rows) & (ri % rows == rows - 1 - ci % rows)).astype(f32)
    turn = turn * jnp.where(ci < own, HELD, 1.0)
    flags = jnp.broadcast_to(blow[...].astype(f32), (8, rows))
    a, b = iota((rows, 128), 0), iota((rows, 128), 1)
    mirror_out[total:total + 8] = place(flags, b == 2 * rows + rows - 1 - a)
    for copy in copies:
        copy.wait()
    pieces = [
        wall_strips(lambda k, c=c: pert[c, :, k, :], PLANES) for c in range(FIELDS)
    ]
    pieces.append(wall_strips(lambda q: coefs[q], 3))
    mirror_out[0:total] = jnp.dot(
        turn, jnp.concatenate(pieces, axis=0),
        precision=lax.Precision.HIGHEST, preferred_element_type=f32,
    )


def pack_strips_kernel(
    rows, me_ref, strips, even_in, odd_in, even_out, odd_out, stage, sems
):
    is_odd = me_ref[0] % 2
    own = rows * FIELDS
    b, a = iota((128, 128), 1), iota((128, 128), 0)
    copies = []
    for p, (out, first) in enumerate(((even_out, 1), (odd_out, 0))):
        parts = [
            head_or_tail(is_odd, strips[c * rows:(c + 1) * rows], first)
            for c in range(FIELDS)
        ]
        parts.append(jnp.zeros((6, 128), f32))
        parts.append(head_or_tail(is_odd, strips[own:own + rows], first))
        parts.append(jnp.zeros((24 - HALO, 128), f32))
        start = jnp.where(is_odd == first, 0, rows - HALO)
        base = own + 2 * HALO - 128
        parts.append(place(
            strips[own + rows:own + rows + 8],
            (b - base == a - 2 * rows - start) & (b >= base) & (b < base + HALO),
        ))
        block = jnp.concatenate(parts, axis=0)
        stage[p, :, 0:128] = block[0:64]
        stage[p, :, 128:256] = block[64:128]
        copy = pltpu.make_async_copy(
            stage.at[p], out.at[pl.ds(PAYLOAD, 64)], sems.at[p]
        )
        copy.start()
        copies.append(copy)
    for copy in copies:
        copy.wait()


def segments(block, hold, store):
    hold[...] = block.T
    for jl in range(32):
        store(jl, hold[pl.ds(jl, SEGMENTS, stride=32), :])


def prepare_kernel(
    rows, me_ref, cxi, ceta, cspan, pert_hbm, ax_hbm, ae_hbm, sp_hbm, blow,
    even_out, odd_out, xt, ct, last_field, wide, narrow,
    pert, coefs, hold, sems,
):
    is_odd = me_ref[0] % 2
    copies = [pltpu.make_async_copy(pert_hbm, pert, sems.at[0])]
    for q, ref in enumerate((ax_hbm, ae_hbm, sp_hbm)):
        copies.append(pltpu.make_async_copy(ref, coefs.at[q], sems.at[1 + q]))
    for copy in copies:
        copy.start()
    own = rows * FIELDS
    slots = rows + HALO
    rc, rs, _ = lane_index((LANES, LANES), 0, rows)
    cc, cs, _ = lane_index((LANES, LANES), 1, rows)
    apart = jnp.where((rs >= 0) & (cs >= 0), (rs - cs + slots) % slots, 0)
    band = jnp.zeros((LANES, LANES), f32)
    for d, value in ((1, 45.0), (2, -9.0), (3, 1.0)):
        band = jnp.where(apart == d, value, band)
        band = jnp.where(apart == slots - d, -value, band)
    same = ((rs == cs) & (rs >= 0)).astype(f32)
    col_comp, _, _ = lane_index((1, LANES), 1, rows)

    def spread(matrix):
        total = jnp.zeros((LANES, LANES), f32)
        for d in range(FIELDS):
            line = jnp.zeros((1, LANES), f32)
            for c in range(FIELDS):
                line = jnp.where(col_comp == c, matrix[c, d], line)
            total = jnp.where(rc == d, line, total)
        return total

    xi = spread(cxi) * band * (-time_step / 60.0)
    eta = spread(ceta) * same * (-time_step * 45.0 / 60.0)
    span = spread(cspan) * same * (-time_step * 0.5)
    grad = jnp.where(rc == cc, band, 0.0)
    for w, first, small in ((xi, 0, 0), (eta, 2, 1), (grad, 4, 2), (span, 5, 3)):
        hi, lo = split(w)
        wide[first * LANES:(first + 1) * LANES] = hi
        if first != 4:
            wide[(first + 1) * LANES:(first + 2) * LANES] = lo
        narrow[small * LANES:(small + 1) * LANES] = w.astype(f8)
    for copy in copies:
        copy.wait()
    a, b = iota((rows, LANES), 0), iota((rows, LANES), 1)
    flags = jnp.broadcast_to(blow[...].astype(f32), (8, rows))
    for out, first in ((even_out, 1), (odd_out, 0)):
        for k in range(PLANES):
            for c in range(FIELDS):
                out[k * 96 + c * HALO:k * 96 + (c + 1) * HALO] = head_or_tail(
                    is_odd, pert[c, :, k, :], first
                ) * HELD
            out[k * 96 + 90:k * 96 + 96] = jnp.zeros((6, LANES), f32)
        for q in range(3):
            out[384 + q * 24:384 + q * 24 + HALO] = head_or_tail(is_odd, coefs[q], first)
            out[384 + q * 24 + HALO:384 + q * 24 + 24] = jnp.zeros((24 - HALO, LANES), f32)
        start = jnp.where(is_odd == first, 0, rows - HALO)
        base = own + 2 * HALO
        out[456:464] = place(flags, (b - base == a - start) & (b >= base) & (b < base + HALO))
        out[PAYLOAD:PAYLOAD + 64] = jnp.zeros((64, LANES), f32)
    for k in range(PLANES):
        block = HELD * jnp.concatenate([pert[c, :, k, :] for c in range(FIELDS - 1)], axis=0)

        def store(jl, slab, k=k):
            xt[k, jl] = slab

        segments(block, hold, store)
        last_field[k] = pert[FIELDS - 1, :, k, :] * HELD
    for q in range(3):
        block = jnp.concatenate([coefs[q] * SCALES[q] + KEEPS[q]] * (FIELDS - 1), axis=0)

        def store(jl, slab, q=q):
            ct[q, jl] = slab

        segments(block, hold, store)


def window_kernel(
    rows, total_rows, second, me_ref, cut_ref, blow, strips, xt, ct, last_field,
    wide, narrow, halo_in, *rest,
):
    if second:
        xe, ge, ce, gce, le = rest[:5]
        out, rest = rest[5], rest[6:]
    else:
        xe, ge, ce, gce, le = rest[:5]
        rest = rest[5:]
    (
        xs, v0, gs, gv, zz, partial, high, low, span_high, span_low,
        coef, gcoef, lanes_ref, wx, wx8, hold,
    ) = rest
    me = me_ref[0]
    is_odd = me % 2
    own = rows * FIELDS
    slots = rows + HALO
    rs = lane_index((LANES, LANES), 0, rows)[1]

    def set_xi_weights(low, high):
        keep = jnp.where((rs >= low) & (rs < high), 0.0, 1.0)
        for source, kept, count, masked in (
            (wide, wx, 7, (0, 1, 4)), (narrow, wx8, 4, (0, 2)),
        ):
            for t in range(count):
                block = source[t * LANES:(t + 1) * LANES]
                if t in masked:
                    block = (block.astype(f32) * keep).astype(block.dtype)
                kept[t * LANES:(t + 1) * LANES] = block

    def dot(a, w):
        return jnp.dot(a, w, preferred_element_type=f32)

    def twice(a):
        return jnp.concatenate([a, a], axis=1)

    def couple_ij(xh, eh, low):
        n = LANES
        first = dot(jnp.concatenate([xh, xh, eh, eh], axis=1), wx[0:4 * n])
        first8 = dot(low, wx8[0:2 * n])
        grad = dot(xh, wx[4 * n:5 * n])
        grad8 = dot(low[:, 0:n], wx8[2 * n:3 * n])
        return first, first8, grad, grad8

    def couple_k(sh, sl):
        n = LANES
        return dot(twice(sh), wx[5 * n:7 * n]) + dot(sl, wx8[3 * n:4 * n])

    comp, slot, is_own = lane_index((1, LANES), 1, rows)
    sign = jnp.where(comp == 2, -1.0, 1.0).astype(f32)
    a, b = iota((rows, LANES), 0), iota((rows, LANES), 1)
    own_flags = place(
        jnp.broadcast_to(blow[...].astype(f32), (8, rows)), b == 2 * rows + a
    )
    own_mirror = jnp.concatenate(
        [strips[own + rows:own + rows + 8], jnp.zeros((8, LANES - 128), f32)], axis=1
    )

    def cut_lanes(g):
        i = me * rows + g - HALO
        mirror = total_rows - 1 - i
        inside = ((i >= cut_ref[0]) & (i < cut_ref[1])) | (
            (mirror >= cut_ref[0]) & (mirror < cut_ref[1])
        )
        return inside.astype(f32)

    def read_window(halo, halo_right):
        for k in range(PLANES):
            xs[k, 3:35, :, 0:128] = xt[k]

            def store(jl, slab, k=k):
                xs[k, 3 + jl, :, 128:256] = slab

            segments(
                jnp.concatenate([last_field[k], halo[k * 96:(k + 1) * 96]], axis=0),
                hold, store,
            )
        for q in range(3):
            coef[q, :, :, 0:128] = ct[q]
            edge = halo[384 + q * 24:384 + q * 24 + HALO] * SCALES[q] + KEEPS[q]
            block = jnp.concatenate(
                [jnp.zeros((rows, LANES), f32)] + [edge] * FIELDS
                + [jnp.zeros((128 - rows - FIELDS * HALO, LANES), f32)], axis=0,
            )
            lane = iota((1, 128), 1)

            def store(jl, slab, q=q):
                coef[q, jl, :, 128:256] = jnp.where(lane < rows, ct[q, jl], slab)

            segments(block, hold, store)
        near, far = halo[PAYLOAD:PAYLOAD + 64, 0:128], halo[PAYLOAD:PAYLOAD + 64, 128:256]
        last = strips[(FIELDS - 1) * rows:own]
        left = strips[0:128].T
        right = jnp.concatenate([last, near, far[0:32]], axis=0).T
        hold[0:128], hold[128:256] = left, right
        for m in range(HALO):
            for t in range(2):
                line = hold[pl.ds(t * 128 + m, PLANES, stride=STRIP), :]
                gs[3 + m, 0:4, t * 128:(t + 1) * 128] = line
                gs[3 + m, 4:8, t * 128:(t + 1) * 128] = line
        mine, edge = strips[own:own + rows], far[32:32 + HALO]
        hold[0:128] = jnp.concatenate([mine] * (FIELDS - 1), axis=0).T
        hold[128:256] = jnp.concatenate(
            [mine] + [edge] * FIELDS
            + [jnp.zeros((128 - rows - FIELDS * HALO, 128), f32)], axis=0,
        ).T
        for q in range(3):
            for m in range(HALO):
                for t in range(2):
                    at = t * 128 + q * STRIP + m
                    gcoef[q, m, :, t * 128:(t + 1) * 128] = jnp.broadcast_to(
                        hold[at:at + 1, :] * SCALES[q] + KEEPS[q], (8, 128)
                    )
        g = jnp.where(is_own, slot, jnp.where(halo_right == 1, slots + slot, slot))
        lanes_ref[0] = jnp.broadcast_to(cut_lanes(g), (8, LANES))
        lanes_ref[1] = 2.0 * (own_flags + halo[456:464])
        lanes_ref[2] = 2.0 * (
            own_mirror + jnp.concatenate([jnp.zeros((8, 128), f32), far[56:64]], axis=1)
        )

    sub = iota((8, LANES), 0)

    def pressure(line):
        near = pltpu.roll(line, LANES - 2 * rows, axis=1)
        far = pltpu.roll(line, LANES - 2 * HALO, axis=1)
        return jnp.where(is_own, near, far)

    def slopes(load, offset):
        return (
            (load(offset + 1) - load(offset - 1))
            - 0.2 * (load(offset + 2) - load(offset - 2))
            + (1.0 / 45.0) * (load(offset + 3) - load(offset - 3))
        )

    def time_stage(depth, alpha, beta):
        cut = lanes_ref[0] > 0.5
        wall = []
        for m in range(3):
            line = jnp.concatenate([xs[k, 3 + m, 0:1, :] for k in range(PLANES)], axis=0)
            wall.append(jnp.concatenate([line, line], axis=0))
        wall_g = [gs[3 + m] for m in range(3)]
        lift = lanes_ref[1] * jnp.where(comp == 2, pressure(wall[0]), 0.0)
        lift_g = lanes_ref[2] * jnp.where(comp == 2, pressure(wall_g[0]), 0.0)
        for m in range(3):
            ghost = jnp.where(cut, sign * wall_g[m], sign * wall[m] + lift)
            gs[2 - m] = jnp.where(cut, sign * wall[m], sign * wall_g[m] + lift_g)
            for k in range(PLANES):
                below = pltpu.roll(xs[k, 34 - m], 1, axis=0)
                xs[k, 2 - m] = jnp.where(sub == 0, ghost[k:k + 1], below)
                above = pltpu.roll(xs[k, 3 + m], SEGMENTS - 1, axis=0)
                xs[k, 35 + m] = jnp.where(sub == SEGMENTS - 1, 0.0, above)
        rows8 = 8 * SEGMENTS
        chunks = [(8 * c, slice(rows8 * c, rows8 * (c + 1))) for c in range(4)]

        def flat(v):
            return v.reshape(rows8, LANES)

        def split_plane(k):
            for at, here in chunks:
                x = flat(xs[k, 3 + at:11 + at])
                e = flat(slopes(lambda o: xs[k, at + o:at + o + 8], 3))
                cb, cd = flat(coef[1, at:at + 8]), flat(coef[2, at:at + 8])
                partial[k, here] = cb * e + cd * x
                xh, xl = split_small(x)
                eh, el = split_small(e)
                high[k, here, 0:LANES] = xh
                high[k, here, LANES:2 * LANES] = eh
                low[k, here, 0:LANES] = xl
                low[k, here, LANES:2 * LANES] = el

        for p in range(2):
            for at, here in chunks:
                s = xs[p + 1, 3 + at:11 + at] - xs[(p + 3) % PLANES, 3 + at:11 + at]
                span_high[p, here], span_low[p, here] = split_small(flat(s))
        split_plane(0)
        for p in range(2):
            zz[p] = couple_k(span_high[p], span_low[p])
        for k in range(PLANES):
            first, first8, grad, grad8 = couple_ij(
                high[k, :, 0:LANES], high[k, :, LANES:2 * LANES], low[k]
            )
            if k + 1 < PLANES:
                split_plane(k + 1)
            for at, here in chunks:
                ca = flat(coef[0, at:at + 8])
                r = (first[here] + first8[here]) + ca * (grad[here] + grad8[here])
                r = r + partial[k, here]
                r = r + zz[k, here] if k < 2 else r - zz[k - 2, here]
                r = alpha * flat(v0[k, at:at + 8]) + beta * r
                xs[k, 3 + at:11 + at] = r.reshape(8, SEGMENTS, LANES)
        n = depth * 8
        x = gs[3:3 + depth].reshape(n, LANES)
        e = slopes(lambda at: gs[at:at + depth], 3).reshape(n, LANES)
        xh, xl = split_small(x)
        eh, el = split_small(-e)
        first, first8, grad, grad8 = couple_ij(xh, eh, jnp.concatenate([xl, el], axis=1))
        s = gs[3:3 + depth]
        s = pltpu.roll(s, 7, axis=1) - pltpu.roll(s, 1, axis=1)
        z = couple_k(*split_small(s.reshape(n, LANES)))
        ca, cb, cd = (gcoef[q, 0:depth].reshape(n, LANES) for q in range(3))
        r = cb * e + cd * x - (first + first8) - ca * (grad + grad8) + z
        gs[3:3 + depth] = alpha * gv[0:depth] + beta * r.reshape(depth, 8, LANES)

    def time_steps(depth):
        for k in range(PLANES):
            v0[k] = xs[k, 3:35]
        gv[0:depth] = gs[3:3 + depth]

        def stage(s, carry):
            alpha = jnp.where(s == 0, 0.0, jnp.where(s == 1, 0.75, 1.0 / 3.0)).astype(f32)
            beta = jnp.where(s == 0, 1.0, jnp.where(s == 1, 0.25, 2.0 / 3.0)).astype(f32)
            time_stage(depth, alpha, beta)
            return carry

        lax.fori_loop(0, 3, stage, 0)

    at_start = me == 0
    at_end = me == total_rows // rows - 1
    gs[...] = jnp.zeros(gs.shape, f32)
    if not second:
        set_xi_weights(0, 0)
        read_window(halo_in, 1 - is_odd)
        time_steps(HALO - 2)
        for k in range(PLANES):
            xe[k] = xs[k, 3:35]
        ge[...] = gs[3:3 + REACH]
        for q in range(3):
            ce[q] = coef[q, :, :, 128:256]
        gce[...] = gcoef[:, 0:REACH]
        le[...] = lanes_ref[...]
        return
    outside = at_start | at_end
    set_xi_weights(0, jnp.where(outside, HALO, 0))
    read_window(halo_in, is_odd)
    time_steps(HALO - 2)
    set_xi_weights(
        jnp.where(at_start, REACH, 0),
        jnp.where(at_start, HALO, jnp.where(at_end, REACH, 0)),
    )
    left = (slot >= REACH) & (slot < REACH + rows)
    from_e = jnp.where(left, is_odd, 1 - is_odd) == 1
    for k in range(PLANES):
        xs[k, 3:35] = jnp.where(from_e, xe[k], xs[k, 3:35])
    gs[3:3 + REACH] = jnp.where(from_e, ge[...], gs[3:3 + REACH])
    coef[:, :, :, 128:256] = jnp.where(from_e[:, 128:256], ce[...], coef[:, :, :, 128:256])
    gcoef[:, 0:REACH] = jnp.where(from_e, gce[...], gcoef[:, 0:REACH])
    g = jnp.where(is_own, slot, jnp.where(slot < REACH, slots + slot, slot))
    lanes_ref[0] = jnp.broadcast_to(cut_lanes(g), (8, LANES))
    lanes_ref[1] = jnp.where(from_e, le[1], lanes_ref[1])
    lanes_ref[2] = jnp.where(from_e, le[2], lanes_ref[2])
    time_steps(REACH - 1)
    for k in range(PLANES):
        for t in range(2):
            for jl in range(32):
                hold[pl.ds(jl, SEGMENTS, stride=32), :] = xs[
                    k, 3 + jl, :, t * 128:(t + 1) * 128
                ]
            block = hold[...].T * (1.0 / HELD)
            for c in range(FIELDS):
                at = c * rows - t * 128
                if 0 <= at < 128:
                    out[c, :, k, :] = block[at:at + rows]


def on_device(
    perturbation, advect_xi, advect_eta, sponge,
    couple_xi, couple_eta, couple_span, wake_cut, blowing,
):
    rows = perturbation.shape[1]
    devices = lax.axis_size("wrap")
    total_rows = rows * devices
    own = rows * FIELDS
    me = lax.axis_index("wrap").astype(jnp.int32).reshape(1)
    flags = blowing.reshape(1, rows)
    mirror = [(i, devices - 1 - i) for i in range(devices)]
    same_chip = [(i, i ^ 1) for i in range(devices)]
    next_chip = [(i, i + 1 if i % 2 else i - 1) for i in range(1, devices - 1)]

    vmem = pl.BlockSpec(memory_space=pltpu.VMEM)
    smem = pl.BlockSpec(memory_space=pltpu.SMEM)
    anywhere = pl.BlockSpec(memory_space=pl.ANY)
    hbm = pl.BlockSpec(memory_space=pltpu.HBM)

    def call(kernel, outs, ins, scratch, us, out_specs=None, vmem_kib=32 * 1024, **more):
        return pl.pallas_call(
            kernel,
            out_shape=outs,
            in_specs=ins,
            out_specs=out_specs or (vmem,) * len(outs),
            scratch_shapes=scratch,
            compiler_params=pltpu.CompilerParams(vmem_limit_bytes=vmem_kib * 1024),
            cost_estimate=pl.CostEstimate(
                flops=int(us * 1e9), bytes_accessed=int(us * 3e6), transcendentals=0
            ),
            **more,
        )

    def shape(*dims, dtype=f32):
        return jax.ShapeDtypeStruct(dims, dtype)

    dma = pltpu.SemaphoreType.DMA
    (to_mirror,) = call(
        functools.partial(pack_mirror_kernel, rows),
        (shape(own + rows + 8, 128),),
        [hbm] * 4 + [vmem],
        [
            pltpu.VMEM((FIELDS, rows, PLANES, 128), f32),
            pltpu.VMEM((3, rows, 128), f32),
            dma((4,)),
        ],
        1,
        vmem_kib=65340,
    )(perturbation, advect_xi, advect_eta, sponge, flags)
    strips = lax.ppermute(to_mirror, "wrap", mirror)

    state = (PLANES, 32, SEGMENTS, LANES)
    payload = shape(PAYLOAD + 64, LANES)
    even, odd, xt, ct, last_field, wide, narrow = call(
        functools.partial(prepare_kernel, rows),
        (
            payload, payload,
            shape(PLANES, 32, SEGMENTS, 128), shape(3, 32, SEGMENTS, 128),
            shape(PLANES, rows, LANES),
            shape(7 * LANES, LANES, dtype=bf16), shape(4 * LANES, LANES, dtype=f8),
        ),
        [smem] * 4 + [hbm] * 4 + [vmem],
        [
            pltpu.VMEM((FIELDS, rows, PLANES, LANES), f32),
            pltpu.VMEM((3, rows, LANES), f32),
            pltpu.VMEM((LANES, 128), f32),
            dma((4,)),
        ],
        4,
    )(
        me, couple_xi, couple_eta, couple_span,
        perturbation, advect_xi, advect_eta, sponge, flags,
    )
    even, odd = call(
        functools.partial(pack_strips_kernel, rows),
        (payload, payload),
        [smem, vmem, anywhere, anywhere],
        [pltpu.VMEM((2, 64, LANES), f32), dma((2,))],
        1,
        out_specs=(anywhere, anywhere),
        input_output_aliases={2: 0, 3: 1},
    )(me, strips, even, odd)
    from_next = lax.ppermute(odd, "wrap", next_chip)
    from_same = lax.ppermute(even, "wrap", same_chip)

    scratch = [
        pltpu.VMEM((PLANES, 38, SEGMENTS, LANES), f32),
        pltpu.VMEM(state, f32),
        pltpu.VMEM((3 + HALO + 3, 8, LANES), f32),
        pltpu.VMEM((HALO, 8, LANES), f32),
        pltpu.VMEM((2, LANES, LANES), f32),
        pltpu.VMEM((PLANES, LANES, LANES), f32),
        pltpu.VMEM((PLANES, LANES, 2 * LANES), bf16),
        pltpu.VMEM((PLANES, LANES, 2 * LANES), f8),
        pltpu.VMEM((2, LANES, LANES), bf16),
        pltpu.VMEM((2, LANES, LANES), f8),
        pltpu.VMEM((3, 32, SEGMENTS, LANES), f32),
        pltpu.VMEM((3, HALO, 8, LANES), f32),
        pltpu.VMEM((3, 8, LANES), f32),
        pltpu.VMEM((7 * LANES, LANES), bf16),
        pltpu.VMEM((4 * LANES, LANES), f8),
        pltpu.VMEM((LANES, 128), f32),
    ]
    common = (me, wake_cut, flags, strips, xt, ct, last_field, wide, narrow)
    specs = [smem, smem] + [vmem] * 7
    first = call(
        functools.partial(window_kernel, rows, total_rows, False),
        (
            shape(*state), shape(REACH, 8, LANES), shape(3, 32, SEGMENTS, 128),
            shape(3, REACH, 8, LANES), shape(3, 8, LANES),
        ),
        specs + [vmem], scratch, 9,
    )(*common, from_same)
    (out,) = call(
        functools.partial(window_kernel, rows, total_rows, True),
        (shape(*perturbation.shape),),
        specs + [vmem] * 6, scratch, 18,
    )(*common, from_next, *first)
    return out


def solution(mesh):
    in_specs = (
        P(None, "wrap", None, None),
        P("wrap", None),
        P("wrap", None),
        P("wrap", None),
        P(),
        P(),
        P(),
        P(),
        P("wrap"),
    )
    out_specs = P(None, "wrap", None, None)
    return jax.shard_map(
        on_device, mesh=mesh, in_specs=in_specs, out_specs=out_specs, check_vma=False
    )
```

time: 65.2 us -> 50.3 us (0.77)
  waiting for transfers between devices: 12.5 us -> 0.77 us
  starting transfers between devices: 20.1 us -> 17.8 us
  local copies, waits for them, and re-layouts: 4.03 us -> 2.38 us
  Pallas kernels: 28.1 us -> 29 us
    ppermute x4 -> x2, starting transfers between devices: 19 us -> 9.07 us  [the longest x1 8.97 us: on_device(): from_next = lax.ppermute(odd, 'wrap', next_chip)]
    ppermute x1, waiting for transfers between devices: 10.6 us -> 0.77 us  [on_device(): strips = lax.ppermute(to_mirror, 'wrap', mirror)]
    ppermute x1, starting transfers between devices: 1.06 us -> 8.76 us  [on_device(): strips = lax.ppermute(to_mirror, 'wrap', mirror)]
    ppermute x4 -> x2, waiting for transfers between devices: 1.93 us -> 0.01 us  [the longest x1 0.01 us: on_device(): from_same = lax.ppermute(even, 'wrap', same_chip)]
    unnamed x20 -> x18, local copies, waits for them, and re-layouts: 4.03 us -> 2.38 us
    pallas_call x3 -> x5, Pallas kernels: 28.1 us -> 29 us  [the longest x1 15.1 us: on_device(): call(functools.partial(window_kernel, rows, total_rows, True), (shape(*pe...]
  transfers between devices with their start and end apart: 5 -> 3, of which waited for: 2 -> 1; matrix products, arithmetic and copies ran while one was open for 0% -> 0% of each run, Pallas kernels for 0% -> 21%
where the time goes in v2:
time: 50.3 us; the launch traced here: 50.1 us
  Pallas kernels  29 us (58%)
  starting transfers between devices  17.8 us (35%)
  local copies, waits for them, and re-layouts  2.38 us (5%)
  waiting for transfers between devices  0.77 us (2%)
    pallas_call x1, Pallas kernels, on_device(): call(functools.partial(window_kernel, rows, total_rows, True), (shape(*pe...  15.1 us
    ppermute x1, starting transfers between devices, on_device(): from_next = lax.ppermute(odd, 'wrap', next_chip)  8.97 us
    ppermute x1, starting transfers between devices, on_device(): strips = lax.ppermute(to_mirror, 'wrap', mirror)  8.76 us
    pallas_call x1, Pallas kernels, on_device(): call(functools.partial(window_kernel, rows, total_rows, False), (shape(*s...  7.35 us
    pallas_call x1, Pallas kernels, on_device(): call(functools.partial(prepare_kernel, rows), (payload, payload, shape(PL...  3.29 us
    pallas_call x1, Pallas kernels, on_device(): call(functools.partial(pack_mirror_kernel, rows), (shape(own + rows + 8,...  2.86 us
    unnamed x18, local copies, waits for them, and re-layouts  2.38 us
  transfers between devices with their start and end apart: 3, of which 1 were waited for; matrix products, arithmetic and copies ran while one was open for 0% of the time, Pallas kernels for 21%

profile of v2, /device:TPU:2, one launch (start us, length us, event | category | flops | bytes accessed | tf_op | source)
XLA Modules:
  0.0 50.1 jit_solution(15506123552410669643)
XLA Ops:
  0.0 0.0 copy-start.1
  0.0 0.0 copy-start.2
  0.0 0.0 copy-start.3
  0.0 0.0 copy-start.5
  0.0 0.0 copy-start.6
  0.0 2.9 %shard_map.91 = f32[200,128]{1,0:T(8,128)} custom-call(f32[5,32,4,256]{3,2,1,0:T(4,128)} %pert_hbm.3, f32[32,256]{1,0:T(8,128)} %ax_hbm.3, f32[32,256]{1,0:T(8,128)} %ae_hbm.3, f32[32,256]{1,0:T(8,128)} %sp_hbm.3, s32[1,32]{1,0:T(1,128)} %bitcast.2), custom_call_target="tpu_custom_call" | custom-call | flops 1000000000 | bytes 3000000 | tf_op jit(solution)/shard_map/pallas_call | solution.py:522
  2.9 0.0 copy-start.4
  2.9 8.8 %collective-permute-start = (f32[200,128]{1,0:T(8,128)}, f32[200,128]{1,0:T(8,128)S(1)}, u32[]{:S(2)}, u32[]{:S(2)}) collective-permute-start(f32[200,128]{1,0:T(8,128)} %shard_map.91), channel_id=1, source_target_pairs={{0,255},{1,254},{2,253},{3,252},{4,251},{5,250},{6,249},{7,248},{8... | collective-permute-start | bytes 307208 | tf_op jit(solution)/shard_map/ppermute | solution.py:534
  11.7 0.0 copy-start.8
  11.7 0.0 copy-done.1
  11.7 0.0 copy-done.2
  11.7 0.0 copy-done.3
  11.7 0.0 copy-done.5
  11.7 0.0 copy-done.6
  11.7 0.0 copy-done.4
  11.7 0.6 %copy-done.8 = s32[32]{0:T(128)S(1)} copy-done((s32[32]{0:T(128)S(1)}, s32[32]{0:T(128)}, u32[]{:S(2)}) %copy-start.8) | copy-done | bytes 152
  12.3 0.0 copy-start
  12.3 1.1 %copy-done = f32[5,32,4,256]{3,2,1,0:T(4,128)S(1)} copy-done((f32[5,32,4,256]{3,2,1,0:T(4,128)S(1)}, f32[5,32,4,256]{3,2,1,0:T(4,128)}, u32[]{:S(2)}) %copy-start) | copy-done | bytes 655384
  13.4 3.3 %shard_map.92 = (f32[528,256]{1,0:T(8,128)S(1)}, f32[528,256]{1,0:T(8,128)S(1)}, f32[4,32,8,128]{3,2,1,0:T(8,128)S(1)}, f32[3,32,8,128]{3,2,1,0:T(8,128)S(1)}, f...) custom-call(s32[1]{0:T(128)} %bitcast.me_ref, f32[5,5]{1,0:T(8,128)S(1)} %copy-done.4, ...), custom_call_target="tpu_custom_call" | custom-call | flops 4000000000 | bytes 12000000 | tf_op jit(solution)/shard_map/pallas_call | solution.py:538
  16.7 0.8 %collective-permute-done.strips = f32[200,128]{1,0:T(8,128)S(1)} collective-permute-done((f32[200,128]{1,0:T(8,128)}, f32[200,128]{1,0:T(8,128)S(1)}, u32[]{:S(2)}, u32[]{:S(2)}) %collective-permute-start) | collective-permute-done | bytes 102432 | tf_op jit(solution)/shard_map/ppermute | solution.py:534
  17.5 0.4 shard_map.93
  17.9 0.1 collective-permute-start.2
  18.0 9.0 %collective-permute-start.1 = (f32[528,256]{1,0:T(8,128)S(1)}, f32[528,256]{1,0:T(8,128)S(1)}, u32[]{:S(2)}, u32[]{:S(2)}) collective-permute-start(f32[528,256]{1,0:T(8,128)S(1)} %get-tuple-element.26), channel_id=1, source_target_pairs={{1,2},{2,1},{3,4},{4,3},{5,6},{6,5},{7,8},{8,7},{9,10},{10,9},{11,... | collective-permute-start | bytes 1622024 | tf_op jit(solution)/shard_map/ppermute | solution.py:567
  27.0 0.0 collective-permute-done.2.halo_in
  27.0 0.0 copy-start.7
  27.0 0.6 %copy-done.7 = s32[2]{0:T(128)S(1)} copy-done((s32[2]{0:T(128)S(1)}, s32[2]{0:T(128)}, u32[]{:S(2)}) %copy-start.7) | copy-done | bytes 32
  27.6 7.4 %shard_map.94 = (f32[4,32,8,256]{3,2,1,0:T(8,128)S(1)}, f32[9,8,256]{2,1,0:T(8,128)S(1)}, f32[3,32,8,128]{3,2,1,0:T(8,128)S(1)}, f32[3,9,8,256]{3,2,1,0:T(8,128)S(1)}, f32[3,8,256]{2,1,0:T(8,128)S(1)}) custom-call(s32[1]{0:T(128)} %bitcast.me_ref, s32[2]{0:T(128)S(1)} %copy-done.7, s32[1,32]{1,0:T(1,128)S(1)} %bitcast.4, ...), custom_call_target="tpu_custom_call" | custom-call | flops 8999999488 | bytes 27000000 | tf_op jit(solution)/shard_map/pallas_call | solution.py:590
  35.0 0.0 collective-permute-done.1.halo_in
  35.0 15.1 %shard_map.95 = f32[5,32,4,256]{3,2,1,0:T(4,128)} custom-call(s32[1]{0:T(128)} %bitcast.me_ref, s32[2]{0:T(128)S(1)} %copy-done.7, s32[1,32]{1,0:T(1,128)S(1)} %bitcast.5, f32[200,128]{1,0:T(8,128)S(1)} %collective-permute-done.strips, f32[4,32,8,128]{3,2,1,0:T(8,128)S(1)} %get-tuple-element.19.xt, f32[3,32,8,128]{3,2,1,0:T(8,128)S(1)} %get-tuple-element.20.ct, ...), custom_call_target="tpu_custom_call" | custom-call | flops 17999998976 | bytes 54000000 | tf_op jit(solution)/shard_map/pallas_call | solution.py:598
Async XLA Ops:
  0.0 11.7 %copy-start.1 = (f32[32,256]{1,0:T(8,128)S(1)}, f32[32,256]{1,0:T(8,128)}, u32[]{:S(2)}) copy-start(f32[32,256]{1,0:T(8,128)} %ax_hbm.3) | copy-start | bytes 98308
  0.0 11.7 %copy-start.2 = (f32[32,256]{1,0:T(8,128)S(1)}, f32[32,256]{1,0:T(8,128)}, u32[]{:S(2)}) copy-start(f32[32,256]{1,0:T(8,128)} %ae_hbm.3) | copy-start | bytes 98308
  0.0 11.7 %copy-start.3 = (f32[32,256]{1,0:T(8,128)S(1)}, f32[32,256]{1,0:T(8,128)}, u32[]{:S(2)}) copy-start(f32[32,256]{1,0:T(8,128)} %sp_hbm.3) | copy-start | bytes 98308
  0.0 11.7 %copy-start.5 = (f32[5,5]{1,0:T(8,128)S(1)}, f32[5,5]{1,0:T(8,128)}, u32[]{:S(2)}) copy-start(f32[5,5]{1,0:T(8,128)} %ceta.1) | copy-start | bytes 304
  0.0 11.7 %copy-start.6 = (f32[5,5]{1,0:T(8,128)S(1)}, f32[5,5]{1,0:T(8,128)}, u32[]{:S(2)}) copy-start(f32[5,5]{1,0:T(8,128)} %cspan.1) | copy-start | bytes 304
  2.9 8.8 %copy-start.4 = (f32[5,5]{1,0:T(8,128)S(1)}, f32[5,5]{1,0:T(8,128)}, u32[]{:S(2)}) copy-start(f32[5,5]{1,0:T(8,128)} %cxi.1) | copy-start | bytes 304
  2.9 14.6 %collective-permute-start = (f32[200,128]{1,0:T(8,128)}, f32[200,128]{1,0:T(8,128)S(1)}, u32[]{:S(2)}, u32[]{:S(2)}) collective-permute-start(f32[200,128]{1,0:T(8,128)} %shard_map.91), channel_id=1, source_target_pairs={{0,255},{1,254},{2,253},{3,252},{4,251},{5,250},{6,249},{7,248},{8... | collective-permute-start | bytes 307208 | tf_op jit(solution)/shard_map/ppermute | solution.py:534
  11.7 0.7 %copy-start.8 = (s32[32]{0:T(128)S(1)}, s32[32]{0:T(128)}, u32[]{:S(2)}) copy-start(s32[32]{0:T(128)} %param.17) | copy-start | bytes 388
  12.3 1.1 %copy-start = (f32[5,32,4,256]{3,2,1,0:T(4,128)S(1)}, f32[5,32,4,256]{3,2,1,0:T(4,128)}, u32[]{:S(2)}) copy-start(f32[5,32,4,256]{3,2,1,0:T(4,128)} %pert_hbm.3) | copy-start | bytes 1966084
  17.9 9.1 %collective-permute-start.2 = (f32[528,256]{1,0:T(8,128)S(1)}, f32[528,256]{1,0:T(8,128)S(1)}, u32[]{:S(2)}, u32[]{:S(2)}) collective-permute-start(f32[528,256]{1,0:T(8,128)S(1)} %get-tuple-element.27), channel_id=1, source_target_pairs={{0,1},{1,0},{2,3},{3,2},{4,5},{5,4},{6,7},{7,6},{8,9},{9,8},{10,11... | collective-permute-start | bytes 1622024 | tf_op jit(solution)/shard_map/ppermute | solution.py:568
  18.0 17.0 %collective-permute-start.1 = (f32[528,256]{1,0:T(8,128)S(1)}, f32[528,256]{1,0:T(8,128)S(1)}, u32[]{:S(2)}, u32[]{:S(2)}) collective-permute-start(f32[528,256]{1,0:T(8,128)S(1)} %get-tuple-element.26), channel_id=1, source_target_pairs={{1,2},{2,1},{3,4},{4,3},{5,6},{6,5},{7,8},{8,7},{9,10},{10,9},{11,... | collective-permute-start | bytes 1622024 | tf_op jit(solution)/shard_map/ppermute | solution.py:567
  27.0 0.7 %copy-start.7 = (s32[2]{0:T(128)S(1)}, s32[2]{0:T(128)}, u32[]{:S(2)}) copy-start(s32[2]{0:T(128)} %cut_ref.3) | copy-start | bytes 28

commit v3 on v2

--- a/solution.py
+++ b/solution.py
@@ -76,29 +76,39 @@
     rows, pert_hbm, ax_hbm, ae_hbm, sp_hbm, blow, mirror_out, pert, coefs, sems
 ):
     near = pl.ds(0, 128)
-    copies = [pltpu.make_async_copy(pert_hbm.at[:, :, :, near], pert, sems.at[0])]
+    copies = [
+        pltpu.make_async_copy(pert_hbm.at[c, :, :, near], pert.at[c], sems.at[c])
+        for c in range(FIELDS)
+    ]
     for q, ref in enumerate((ax_hbm, ae_hbm, sp_hbm)):
-        copies.append(pltpu.make_async_copy(ref.at[:, near], coefs.at[q], sems.at[1 + q]))
+        copies.append(
+            pltpu.make_async_copy(ref.at[:, near], coefs.at[q], sems.at[FIELDS + q])
+        )
     for copy in copies:
         copy.start()
     own = rows * FIELDS
     total = own + rows
-    ri, ci = iota((total, total), 0), iota((total, total), 1)
-    turn = ((ri // rows == ci // rows) & (ri % rows == rows - 1 - ci % rows)).astype(f32)
-    turn = turn * jnp.where(ci < own, HELD, 1.0)
+    sub = iota((8, 128), 0)
+
+    def reverse(block):
+        groups = []
+        for at in range(0, rows, 8):
+            x = pltpu.roll(block[at:at + 8], 4, axis=0)
+            for d in (2, 1):
+                up, down = pltpu.roll(x, d, axis=0), pltpu.roll(x, 8 - d, axis=0)
+                x = jnp.where((sub & d) != 0, up, down)
+            groups.append(x)
+        return jnp.concatenate(groups[::-1], axis=0)
+
     flags = jnp.broadcast_to(blow[...].astype(f32), (8, rows))
     a, b = iota((rows, 128), 0), iota((rows, 128), 1)
     mirror_out[total:total + 8] = place(flags, b == 2 * rows + rows - 1 - a)
     for copy in copies:
         copy.wait()
-    pieces = [
-        wall_strips(lambda k, c=c: pert[c, :, k, :], PLANES) for c in range(FIELDS)
-    ]
-    pieces.append(wall_strips(lambda q: coefs[q], 3))
-    mirror_out[0:total] = jnp.dot(
-        turn, jnp.concatenate(pieces, axis=0),
-        precision=lax.Precision.HIGHEST, preferred_element_type=f32,
-    )
+    for c in range(FIELDS):
+        block = wall_strips(lambda k, c=c: pert[c, :, k, :], PLANES)
+        mirror_out[c * rows:(c + 1) * rows] = reverse(block) * HELD
+    mirror_out[own:total] = reverse(wall_strips(lambda q: coefs[q], 3))
 
 
 def pack_strips_kernel(
@@ -134,16 +144,34 @@
         copy.wait()
 
 
-def segments(block, hold, store):
+def segments(block, hold, mid, store):
     hold[...] = block.T
-    for jl in range(32):
-        store(jl, hold[pl.ds(jl, SEGMENTS, stride=32), :])
+    for js in range(SEGMENTS):
+        for low in range(4):
+            mid[low * 64 + js * 8:low * 64 + js * 8 + 8] = hold[
+                pl.ds(js * 32 + low, 8, stride=4), :
+            ]
+    for low in range(4):
+        for part in range(8):
+            store(part * 4 + low, mid[pl.ds(low * 64 + part, SEGMENTS, stride=8), :])
+
+
+def from_segments(load, hold, mid):
+    for low in range(4):
+        for part in range(8):
+            mid[pl.ds(low * 64 + part, SEGMENTS, stride=8), :] = load(part * 4 + low)
+    for js in range(SEGMENTS):
+        for low in range(4):
+            hold[pl.ds(js * 32 + low, 8, stride=4), :] = mid[
+                low * 64 + js * 8:low * 64 + js * 8 + 8
+            ]
+    return hold[...].T
 
 
 def prepare_kernel(
-    rows, me_ref, cxi, ceta, cspan, pert_hbm, ax_hbm, ae_hbm, sp_hbm, blow,
-    even_out, odd_out, xt, ct, last_field, wide, narrow,
-    pert, coefs, hold, sems,
+    rows, me_ref, cut_ref, cxi, ceta, cspan, pert_hbm, ax_hbm, ae_hbm, sp_hbm, blow,
+    even_out, odd_out, xt, ct, last_field, wide, narrow, cuts,
+    pert, coefs, hold, mid, sems,
 ):
     is_odd = me_ref[0] % 2
     copies = [pltpu.make_async_copy(pert_hbm, pert, sems.at[0])]
@@ -152,6 +180,7 @@
     for copy in copies:
         copy.start()
     own = rows * FIELDS
+    cuts[...] = jnp.where(iota((8, 128), 0) == 0, cut_ref[0], cut_ref[1])
     slots = rows + HALO
     rc, rs, _ = lane_index((LANES, LANES), 0, rows)
     cc, cs, _ = lane_index((LANES, LANES), 1, rows)
@@ -206,7 +235,7 @@
         def store(jl, slab, k=k):
             xt[k, jl] = slab
 
-        segments(block, hold, store)
+        segments(block, hold.at[k], mid.at[k], store)
         last_field[k] = pert[FIELDS - 1, :, k, :] * HELD
     for q in range(3):
         block = jnp.concatenate([coefs[q] * SCALES[q] + KEEPS[q]] * (FIELDS - 1), axis=0)
@@ -214,12 +243,12 @@
         def store(jl, slab, q=q):
             ct[q, jl] = slab
 
-        segments(block, hold, store)
+        segments(block, hold.at[PLANES + q], mid.at[PLANES + q], store)
 
 
 def window_kernel(
-    rows, total_rows, second, me_ref, cut_ref, blow, strips, xt, ct, last_field,
-    wide, narrow, halo_in, *rest,
+    rows, total_rows, second, me_ref, blow, strips, xt, ct, last_field,
+    wide, narrow, cuts, halo_in, *rest,
 ):
     if second:
         xe, ge, ce, gce, le = rest[:5]
@@ -229,7 +258,7 @@
         rest = rest[5:]
     (
         xs, v0, gs, gv, zz, partial, high, low, span_high, span_low,
-        coef, gcoef, lanes_ref, wx, wx8, hold,
+        coef, gcoef, lanes_ref, wx, wx8, hold, mid, ghold,
     ) = rest
     me = me_ref[0]
     is_odd = me % 2
@@ -239,14 +268,10 @@
 
     def set_xi_weights(low, high):
         keep = jnp.where((rs >= low) & (rs < high), 0.0, 1.0)
-        for source, kept, count, masked in (
-            (wide, wx, 7, (0, 1, 4)), (narrow, wx8, 4, (0, 2)),
-        ):
-            for t in range(count):
+        for source, kept, masked in ((wide, wx, (0, 1, 4)), (narrow, wx8, (0, 2))):
+            for t in masked:
                 block = source[t * LANES:(t + 1) * LANES]
-                if t in masked:
-                    block = (block.astype(f32) * keep).astype(block.dtype)
-                kept[t * LANES:(t + 1) * LANES] = block
+                kept[t * LANES:(t + 1) * LANES] = (block.astype(f32) * keep).astype(block.dtype)
 
     def dot(a, w):
         return jnp.dot(a, w, preferred_element_type=f32)
@@ -279,21 +304,22 @@
     def cut_lanes(g):
         i = me * rows + g - HALO
         mirror = total_rows - 1 - i
-        inside = ((i >= cut_ref[0]) & (i < cut_ref[1])) | (
-            (mirror >= cut_ref[0]) & (mirror < cut_ref[1])
-        )
+        low, high = cuts[0:1, 0:1], cuts[1:2, 0:1]
+        inside = ((i >= low) & (i < high)) | ((mirror >= low) & (mirror < high))
         return inside.astype(f32)
 
     def read_window(halo, halo_right):
         for k in range(PLANES):
             xs[k, 3:35, :, 0:128] = xt[k]
+            v0[k, :, :, 0:128] = xt[k]
 
             def store(jl, slab, k=k):
                 xs[k, 3 + jl, :, 128:256] = slab
+                v0[k, jl, :, 128:256] = slab
 
             segments(
                 jnp.concatenate([last_field[k], halo[k * 96:(k + 1) * 96]], axis=0),
-                hold, store,
+                hold.at[k], mid.at[k], store,
             )
         for q in range(3):
             coef[q, :, :, 0:128] = ct[q]
@@ -307,20 +333,22 @@
             def store(jl, slab, q=q):
                 coef[q, jl, :, 128:256] = jnp.where(lane < rows, ct[q, jl], slab)
 
-            segments(block, hold, store)
+            segments(block, hold.at[PLANES + q], mid.at[PLANES + q], store)
         near, far = halo[PAYLOAD:PAYLOAD + 64, 0:128], halo[PAYLOAD:PAYLOAD + 64, 128:256]
         last = strips[(FIELDS - 1) * rows:own]
         left = strips[0:128].T
         right = jnp.concatenate([last, near, far[0:32]], axis=0).T
-        hold[0:128], hold[128:256] = left, right
+        ghold[0, 0:128], ghold[0, 128:256] = left, right
         for m in range(HALO):
             for t in range(2):
-                line = hold[pl.ds(t * 128 + m, PLANES, stride=STRIP), :]
+                line = ghold[0, pl.ds(t * 128 + m, PLANES, stride=STRIP), :]
                 gs[3 + m, 0:4, t * 128:(t + 1) * 128] = line
                 gs[3 + m, 4:8, t * 128:(t + 1) * 128] = line
+                gv[m, 0:4, t * 128:(t + 1) * 128] = line
+                gv[m, 4:8, t * 128:(t + 1) * 128] = line
         mine, edge = strips[own:own + rows], far[32:32 + HALO]
-        hold[0:128] = jnp.concatenate([mine] * (FIELDS - 1), axis=0).T
-        hold[128:256] = jnp.concatenate(
+        ghold[1, 0:128] = jnp.concatenate([mine] * (FIELDS - 1), axis=0).T
+        ghold[1, 128:256] = jnp.concatenate(
             [mine] + [edge] * FIELDS
             + [jnp.zeros((128 - rows - FIELDS * HALO, 128), f32)], axis=0,
         ).T
@@ -329,7 +357,7 @@
                 for t in range(2):
                     at = t * 128 + q * STRIP + m
                     gcoef[q, m, :, t * 128:(t + 1) * 128] = jnp.broadcast_to(
-                        hold[at:at + 1, :] * SCALES[q] + KEEPS[q], (8, 128)
+                        ghold[1, at:at + 1, :] * SCALES[q] + KEEPS[q], (8, 128)
                     )
         g = jnp.where(is_own, slot, jnp.where(halo_right == 1, slots + slot, slot))
         lanes_ref[0] = jnp.broadcast_to(cut_lanes(g), (8, LANES))
@@ -422,10 +450,6 @@
         gs[3:3 + depth] = alpha * gv[0:depth] + beta * r.reshape(depth, 8, LANES)
 
     def time_steps(depth):
-        for k in range(PLANES):
-            v0[k] = xs[k, 3:35]
-        gv[0:depth] = gs[3:3 + depth]
-
         def stage(s, carry):
             alpha = jnp.where(s == 0, 0.0, jnp.where(s == 1, 0.75, 1.0 / 3.0)).astype(f32)
             beta = jnp.where(s == 0, 1.0, jnp.where(s == 1, 0.25, 2.0 / 3.0)).astype(f32)
@@ -438,7 +462,8 @@
     at_end = me == total_rows // rows - 1
     gs[...] = jnp.zeros(gs.shape, f32)
     if not second:
-        set_xi_weights(0, 0)
+        wx[...] = wide[...]
+        wx8[...] = narrow[...]
         read_window(halo_in, 1 - is_odd)
         time_steps(HALO - 2)
         for k in range(PLANES):
@@ -450,18 +475,28 @@
         le[...] = lanes_ref[...]
         return
     outside = at_start | at_end
-    set_xi_weights(0, jnp.where(outside, HALO, 0))
+    wx[...] = wide[...]
+    wx8[...] = narrow[...]
+
+    @pl.when(outside)
+    def _():
+        set_xi_weights(0, HALO)
+
     read_window(halo_in, is_odd)
     time_steps(HALO - 2)
-    set_xi_weights(
-        jnp.where(at_start, REACH, 0),
-        jnp.where(at_start, HALO, jnp.where(at_end, REACH, 0)),
-    )
+    @pl.when(outside)
+    def _():
+        set_xi_weights(jnp.where(at_start, REACH, 0), jnp.where(at_start, HALO, REACH))
+
     left = (slot >= REACH) & (slot < REACH + rows)
     from_e = jnp.where(left, is_odd, 1 - is_odd) == 1
     for k in range(PLANES):
-        xs[k, 3:35] = jnp.where(from_e, xe[k], xs[k, 3:35])
-    gs[3:3 + REACH] = jnp.where(from_e, ge[...], gs[3:3 + REACH])
+        merged = jnp.where(from_e, xe[k], xs[k, 3:35])
+        xs[k, 3:35] = merged
+        v0[k] = merged
+    merged = jnp.where(from_e, ge[...], gs[3:3 + REACH])
+    gs[3:3 + REACH] = merged
+    gv[0:REACH] = merged
     coef[:, :, :, 128:256] = jnp.where(from_e[:, 128:256], ce[...], coef[:, :, :, 128:256])
     gcoef[:, 0:REACH] = jnp.where(from_e, gce[...], gcoef[:, 0:REACH])
     g = jnp.where(is_own, slot, jnp.where(slot < REACH, slots + slot, slot))
@@ -470,16 +505,23 @@
     lanes_ref[2] = jnp.where(from_e, le[2], lanes_ref[2])
     time_steps(REACH - 1)
     for k in range(PLANES):
-        for t in range(2):
-            for jl in range(32):
-                hold[pl.ds(jl, SEGMENTS, stride=32), :] = xs[
-                    k, 3 + jl, :, t * 128:(t + 1) * 128
-                ]
-            block = hold[...].T * (1.0 / HELD)
-            for c in range(FIELDS):
-                at = c * rows - t * 128
-                if 0 <= at < 128:
-                    out[c, :, k, :] = block[at:at + rows]
+        block = from_segments(
+            lambda jl: xs[k, 3 + jl, :, 0:128], hold.at[k], mid.at[k]
+        ) * (1.0 / HELD)
+        for c in range(FIELDS - 1):
+            out[c, :, k, :] = block[c * rows:(c + 1) * rows]
+    lane = iota((1, 128), 1)
+
+    def last_lanes(jl):
+        line = xs[0, 3 + jl, :, 128:256]
+        for k in range(1, PLANES):
+            moved = pltpu.roll(xs[k, 3 + jl, :, 128:256], k * rows, axis=1)
+            line = jnp.where(lane >= k * rows, moved, line)
+        return line
+
+    block = from_segments(last_lanes, hold.at[PLANES], mid.at[PLANES]) * (1.0 / HELD)
+    for k in range(PLANES):
+        out[FIELDS - 1, :, k, :] = block[k * rows:(k + 1) * rows]
 
 
 def on_device(
@@ -498,8 +540,8 @@
 
     vmem = pl.BlockSpec(memory_space=pltpu.VMEM)
     smem = pl.BlockSpec(memory_space=pltpu.SMEM)
+    hbm = pl.BlockSpec(memory_space=pltpu.HBM)
     anywhere = pl.BlockSpec(memory_space=pl.ANY)
-    hbm = pl.BlockSpec(memory_space=pltpu.HBM)
 
     def call(kernel, outs, ins, scratch, us, out_specs=None, vmem_kib=32 * 1024, **more):
         return pl.pallas_call(
@@ -526,33 +568,35 @@
         [
             pltpu.VMEM((FIELDS, rows, PLANES, 128), f32),
             pltpu.VMEM((3, rows, 128), f32),
-            dma((4,)),
+            dma((FIELDS + 3,)),
         ],
         1,
-        vmem_kib=65340,
+        vmem_kib=64600,
     )(perturbation, advect_xi, advect_eta, sponge, flags)
     strips = lax.ppermute(to_mirror, "wrap", mirror)
 
     state = (PLANES, 32, SEGMENTS, LANES)
     payload = shape(PAYLOAD + 64, LANES)
-    even, odd, xt, ct, last_field, wide, narrow = call(
+    even, odd, xt, ct, last_field, wide, narrow, cuts = call(
         functools.partial(prepare_kernel, rows),
         (
             payload, payload,
             shape(PLANES, 32, SEGMENTS, 128), shape(3, 32, SEGMENTS, 128),
             shape(PLANES, rows, LANES),
             shape(7 * LANES, LANES, dtype=bf16), shape(4 * LANES, LANES, dtype=f8),
+            shape(8, 128, dtype=jnp.int32),
         ),
-        [smem] * 4 + [hbm] * 4 + [vmem],
+        [smem] * 5 + [hbm] * 4 + [vmem],
         [
             pltpu.VMEM((FIELDS, rows, PLANES, LANES), f32),
             pltpu.VMEM((3, rows, LANES), f32),
-            pltpu.VMEM((LANES, 128), f32),
+            pltpu.VMEM((PLANES + 3, LANES, 128), f32),
+            pltpu.VMEM((PLANES + 3, LANES, 128), f32),
             dma((4,)),
         ],
         4,
     )(
-        me, couple_xi, couple_eta, couple_span,
+        me, wake_cut, couple_xi, couple_eta, couple_span,
         perturbation, advect_xi, advect_eta, sponge, flags,
     )
     even, odd = call(
@@ -583,22 +627,24 @@
         pltpu.VMEM((3, 8, LANES), f32),
         pltpu.VMEM((7 * LANES, LANES), bf16),
         pltpu.VMEM((4 * LANES, LANES), f8),
-        pltpu.VMEM((LANES, 128), f32),
+        pltpu.VMEM((PLANES + 3, LANES, 128), f32),
+        pltpu.VMEM((PLANES + 3, LANES, 128), f32),
+        pltpu.VMEM((2, LANES, 128), f32),
     ]
-    common = (me, wake_cut, flags, strips, xt, ct, last_field, wide, narrow)
-    specs = [smem, smem] + [vmem] * 7
+    common = (me, flags, strips, xt, ct, last_field, wide, narrow, cuts)
+    specs = [smem] + [vmem] * 8
     first = call(
         functools.partial(window_kernel, rows, total_rows, False),
         (
             shape(*state), shape(REACH, 8, LANES), shape(3, 32, SEGMENTS, 128),
             shape(3, REACH, 8, LANES), shape(3, 8, LANES),
         ),
-        specs + [vmem], scratch, 9,
+        specs + [vmem], scratch, 8,
     )(*common, from_same)
     (out,) = call(
         functools.partial(window_kernel, rows, total_rows, True),
         (shape(*perturbation.shape),),
-        specs + [vmem] * 6, scratch, 18,
+        specs + [vmem] * 6, scratch, 14,
     )(*common, from_next, *first)
     return out
 

time: 50.3 us -> 47 us (0.934)
  Pallas kernels: 29 us -> 25.4 us
  waiting for transfers between devices: 0.77 us -> 2.96 us
  local copies, waits for them, and re-layouts: 2.38 us -> 0.64 us
    pallas_call x1, Pallas kernels: 15.1 us -> 13.2 us  [on_device(): call(functools.partial(window_kernel, rows, total_rows, True), (shape(*pe...]
    unnamed x18, local copies, waits for them, and re-layouts: 2.38 us -> 0.64 us
    ppermute x1, waiting for transfers between devices: 0.77 us -> 2.26 us  [on_device(): strips = lax.ppermute(to_mirror, 'wrap', mirror)]
    pallas_call x1, Pallas kernels: 7.35 us -> 6.31 us  [on_device(): call(functools.partial(window_kernel, rows, total_rows, False), (shape(*s...]
    ppermute x1, waiting for transfers between devices: 0.01 us -> 0.7 us  [on_device(): from_next = lax.ppermute(odd, 'wrap', next_chip)]
  transfers between devices with their start and end apart: 3 -> 3, of which waited for: 1 -> 2; matrix products, arithmetic and copies ran while one was open for 0% -> 0% of each run, Pallas kernels for 21% -> 20%
where the time goes in v3:
time: 47 us; the launch traced here: 46.8 us
  Pallas kernels  25.4 us (54%)
  starting transfers between devices  17.6 us (37%)
  waiting for transfers between devices  2.96 us (6%)
  local copies, waits for them, and re-layouts  0.64 us (1%)
    pallas_call x1, Pallas kernels, on_device(): call(functools.partial(window_kernel, rows, total_rows, True), (shape(*pe...  13.2 us
    ppermute x1, starting transfers between devices, on_device(): from_next = lax.ppermute(odd, 'wrap', next_chip)  8.8 us
    ppermute x1, starting transfers between devices, on_device(): strips = lax.ppermute(to_mirror, 'wrap', mirror)  8.76 us
    pallas_call x1, Pallas kernels, on_device(): call(functools.partial(window_kernel, rows, total_rows, False), (shape(*s...  6.31 us
    pallas_call x1, Pallas kernels, on_device(): call(functools.partial(prepare_kernel, rows), (payload, payload, shape(PL...  2.87 us
    pallas_call x1, Pallas kernels, on_device(): call(functools.partial(pack_mirror_kernel, rows), (shape(own + rows + 8,...  2.61 us
    ppermute x1, waiting for transfers between devices, on_device(): strips = lax.ppermute(to_mirror, 'wrap', mirror)  2.26 us
  transfers between devices with their start and end apart: 3, of which 2 were waited for; matrix products, arithmetic and copies ran while one was open for 0% of the time, Pallas kernels for 20%

profile of v3, /device:TPU:2, one launch (start us, length us, event | category | flops | bytes accessed | tf_op | source)
XLA Modules:
  0.0 46.8 jit_solution(4782969711179922101)
XLA Ops:
  0.0 0.0 copy-start
  0.0 0.0 copy-start.1
  0.0 0.0 copy-start.2
  0.0 0.0 copy-start.3
  0.0 0.0 copy-start.5
  0.0 0.0 copy-start.6
  0.0 2.6 %shard_map.91 = f32[200,128]{1,0:T(8,128)} custom-call(f32[5,32,4,256]{3,2,1,0:T(4,128)} %pert_hbm.3, f32[32,256]{1,0:T(8,128)} %ax_hbm.3, f32[32,256]{1,0:T(8,128)} %ae_hbm.3, f32[32,256]{1,0:T(8,128)} %sp_hbm.3, s32[1,32]{1,0:T(1,128)} %bitcast.2), custom_call_target="tpu_custom_call" | custom-call | flops 1000000000 | bytes 3000000 | tf_op jit(solution)/shard_map/pallas_call | solution.py:564
  2.7 0.0 copy-start.4
  2.7 8.8 %collective-permute-start = (f32[200,128]{1,0:T(8,128)}, f32[200,128]{1,0:T(8,128)S(1)}, u32[]{:S(2)}, u32[]{:S(2)}) collective-permute-start(f32[200,128]{1,0:T(8,128)} %shard_map.91), channel_id=1, source_target_pairs={{0,255},{1,254},{2,253},{3,252},{4,251},{5,250},{6,249},{7,248},{8... | collective-permute-start | bytes 307208 | tf_op jit(solution)/shard_map/ppermute | solution.py:576
  11.4 0.0 copy-start.7
  11.4 0.0 copy-start.8
  11.4 0.0 copy-done
  11.4 0.0 copy-done.1
  11.4 0.0 copy-done.2
  11.5 0.0 copy-done.3
  11.5 0.0 copy-done.5
  11.5 0.0 copy-done.6
  11.5 0.0 copy-done.4
  11.5 0.6 %copy-done.7 = s32[2]{0:T(128)S(1)} copy-done((s32[2]{0:T(128)S(1)}, s32[2]{0:T(128)}, u32[]{:S(2)}) %copy-start.7) | copy-done | bytes 32
  12.1 0.0 copy-done.8
  12.1 2.9 %shard_map.92 = (f32[528,256]{1,0:T(8,128)S(1)}, f32[528,256]{1,0:T(8,128)S(1)}, f32[4,32,8,128]{3,2,1,0:T(8,128)S(1)}, f32[3,32,8,128]{3,2,1,0:T(8,128)S(1)}, f...) custom-call(s32[1]{0:T(128)} %bitcast.me_ref, ...), custom_call_target="tpu_custom_call" | custom-call | flops 4000000000 | bytes 12000000 | tf_op jit(solution)/shard_map/pallas_call | solution.py:580
  15.0 2.3 %collective-permute-done.strips = f32[200,128]{1,0:T(8,128)S(1)} collective-permute-done((f32[200,128]{1,0:T(8,128)}, f32[200,128]{1,0:T(8,128)S(1)}, u32[]{:S(2)}, u32[]{:S(2)}) %collective-permute-start) | collective-permute-done | bytes 102432 | tf_op jit(solution)/shard_map/ppermute | solution.py:576
  17.2 0.4 shard_map.93
  17.6 0.1 collective-permute-start.2
  17.7 8.8 %collective-permute-start.1 = (f32[528,256]{1,0:T(8,128)S(1)}, f32[528,256]{1,0:T(8,128)S(1)}, u32[]{:S(2)}, u32[]{:S(2)}) collective-permute-start(f32[528,256]{1,0:T(8,128)S(1)} %get-tuple-element.28), channel_id=1, source_target_pairs={{1,2},{2,1},{3,4},{4,3},{5,6},{6,5},{7,8},{8,7},{9,10},{10,9},{11,... | collective-permute-start | bytes 1622024 | tf_op jit(solution)/shard_map/ppermute | solution.py:611
  26.6 0.0 collective-permute-done.2.halo_in
  26.6 6.3 %shard_map.94 = (f32[4,32,8,256]{3,2,1,0:T(8,128)S(1)}, f32[9,8,256]{2,1,0:T(8,128)S(1)}, f32[3,32,8,128]{3,2,1,0:T(8,128)S(1)}, f32[3,9,8,256]{3,2,1,0:T(8,128)S(1)}, f32[3,8,256]{2,1,0:T(8,128)S(1)}) custom-call(s32[1]{0:T(128)} %bitcast.me_ref, s32[1,32]{1,0:T(1,128)S(1)} %bitcast.4, f32[200,128]{1,0:T(8,128)S(1)} %collective-permute-done.strips, ...), custom_call_target="tpu_custom_call" | custom-call | flops 8000000000 | bytes 24000000 | tf_op jit(solution)/shard_map/pallas_call | solution.py:636
  32.9 0.7 %collective-permute-done.1.halo_in = f32[528,256]{1,0:T(8,128)S(1)} collective-permute-done((f32[528,256]{1,0:T(8,128)S(1)}, f32[528,256]{1,0:T(8,128)S(1)}, u32[]{:S(2)}, u32[]{:S(2)}) %collective-permute-start.1) | collective-permute-done | bytes 540704 | tf_op jit(solution)/shard_map/ppermute | solution.py:611
  33.6 13.2 %shard_map.95 = f32[5,32,4,256]{3,2,1,0:T(4,128)} custom-call(s32[1]{0:T(128)} %bitcast.me_ref, s32[1,32]{1,0:T(1,128)S(1)} %bitcast.5, f32[200,128]{1,0:T(8,128)S(1)} %collective-permute-done.strips, f32[4,32,8,128]{3,2,1,0:T(8,128)S(1)} %get-tuple-element.20.xt, f32[3,32,8,128]{3,2,1,0:T(8,128)S(1)} %get-tuple-element.21.ct, ...), custom_call_target="tpu_custom_call" | custom-call | flops 14000000000 | bytes 42000000 | tf_op jit(solution)/shard_map/pallas_call | solution.py:644
Async XLA Ops:
  0.0 11.4 %copy-start = (f32[5,32,4,256]{3,2,1,0:T(4,128)S(1)}, f32[5,32,4,256]{3,2,1,0:T(4,128)}, u32[]{:S(2)}) copy-start(f32[5,32,4,256]{3,2,1,0:T(4,128)} %pert_hbm.3) | copy-start | bytes 1966084
  0.0 11.4 %copy-start.1 = (f32[32,256]{1,0:T(8,128)S(1)}, f32[32,256]{1,0:T(8,128)}, u32[]{:S(2)}) copy-start(f32[32,256]{1,0:T(8,128)} %ax_hbm.3) | copy-start | bytes 98308
  0.0 11.4 %copy-start.2 = (f32[32,256]{1,0:T(8,128)S(1)}, f32[32,256]{1,0:T(8,128)}, u32[]{:S(2)}) copy-start(f32[32,256]{1,0:T(8,128)} %ae_hbm.3) | copy-start | bytes 98308
  0.0 11.4 %copy-start.3 = (f32[32,256]{1,0:T(8,128)S(1)}, f32[32,256]{1,0:T(8,128)}, u32[]{:S(2)}) copy-start(f32[32,256]{1,0:T(8,128)} %sp_hbm.3) | copy-start | bytes 98308
  0.0 11.4 %copy-start.5 = (f32[5,5]{1,0:T(8,128)S(1)}, f32[5,5]{1,0:T(8,128)}, u32[]{:S(2)}) copy-start(f32[5,5]{1,0:T(8,128)} %ceta.1) | copy-start | bytes 304
  0.0 11.4 %copy-start.6 = (f32[5,5]{1,0:T(8,128)S(1)}, f32[5,5]{1,0:T(8,128)}, u32[]{:S(2)}) copy-start(f32[5,5]{1,0:T(8,128)} %cspan.1) | copy-start | bytes 304
  2.7 8.8 %copy-start.4 = (f32[5,5]{1,0:T(8,128)S(1)}, f32[5,5]{1,0:T(8,128)}, u32[]{:S(2)}) copy-start(f32[5,5]{1,0:T(8,128)} %cxi.1) | copy-start | bytes 304
  2.7 14.6 %collective-permute-start = (f32[200,128]{1,0:T(8,128)}, f32[200,128]{1,0:T(8,128)S(1)}, u32[]{:S(2)}, u32[]{:S(2)}) collective-permute-start(f32[200,128]{1,0:T(8,128)} %shard_map.91), channel_id=1, source_target_pairs={{0,255},{1,254},{2,253},{3,252},{4,251},{5,250},{6,249},{7,248},{8... | collective-permute-start | bytes 307208 | tf_op jit(solution)/shard_map/ppermute | solution.py:576
  11.4 0.7 %copy-start.7 = (s32[2]{0:T(128)S(1)}, s32[2]{0:T(128)}, u32[]{:S(2)}) copy-start(s32[2]{0:T(128)} %cut_ref.1) | copy-start | bytes 28
  11.4 0.7 %copy-start.8 = (s32[32]{0:T(128)S(1)}, s32[32]{0:T(128)}, u32[]{:S(2)}) copy-start(s32[32]{0:T(128)} %param.17) | copy-start | bytes 388
  17.6 8.9 %collective-permute-start.2 = (f32[528,256]{1,0:T(8,128)S(1)}, f32[528,256]{1,0:T(8,128)S(1)}, u32[]{:S(2)}, u32[]{:S(2)}) collective-permute-start(f32[528,256]{1,0:T(8,128)S(1)} %get-tuple-element.29), channel_id=1, source_target_pairs={{0,1},{1,0},{2,3},{3,2},{4,5},{5,4},{6,7},{7,6},{8,9},{9,8},{10,11... | collective-permute-start | bytes 1622024 | tf_op jit(solution)/shard_map/ppermute | solution.py:612
  17.7 15.8 %collective-permute-start.1 = (f32[528,256]{1,0:T(8,128)S(1)}, f32[528,256]{1,0:T(8,128)S(1)}, u32[]{:S(2)}, u32[]{:S(2)}) collective-permute-start(f32[528,256]{1,0:T(8,128)S(1)} %get-tuple-element.28), channel_id=1, source_target_pairs={{1,2},{2,1},{3,4},{4,3},{5,6},{6,5},{7,8},{8,7},{9,10},{10,9},{11,... | collective-permute-start | bytes 1622024 | tf_op jit(solution)/shard_map/ppermute | solution.py:611

commit v4 on v3

--- a/solution.py
+++ b/solution.py
@@ -18,7 +18,10 @@
 PLANES = 4
 SEGMENTS = 8
 
-PAYLOAD = 464
+EDGE = 90
+COEFS = 360
+FLAGS = 416
+PAYLOAD = 424
 SCALES = (-time_step / 60.0, -time_step * 45.0 / 60.0, -time_step)
 KEEPS = (0.0, 0.0, 1.0)
 
@@ -218,16 +221,15 @@
     for out, first in ((even_out, 1), (odd_out, 0)):
         for k in range(PLANES):
             for c in range(FIELDS):
-                out[k * 96 + c * HALO:k * 96 + (c + 1) * HALO] = head_or_tail(
+                out[k * EDGE + c * HALO:k * EDGE + (c + 1) * HALO] = head_or_tail(
                     is_odd, pert[c, :, k, :], first
                 ) * HELD
-            out[k * 96 + 90:k * 96 + 96] = jnp.zeros((6, LANES), f32)
         for q in range(3):
-            out[384 + q * 24:384 + q * 24 + HALO] = head_or_tail(is_odd, coefs[q], first)
-            out[384 + q * 24 + HALO:384 + q * 24 + 24] = jnp.zeros((24 - HALO, LANES), f32)
+            out[COEFS + q * HALO:COEFS + (q + 1) * HALO] = head_or_tail(is_odd, coefs[q], first)
+        out[COEFS + 3 * HALO:FLAGS] = jnp.zeros((FLAGS - COEFS - 3 * HALO, LANES), f32)
         start = jnp.where(is_odd == first, 0, rows - HALO)
         base = own + 2 * HALO
-        out[456:464] = place(flags, (b - base == a - start) & (b >= base) & (b < base + HALO))
+        out[FLAGS:PAYLOAD] = place(flags, (b - base == a - start) & (b >= base) & (b < base + HALO))
         out[PAYLOAD:PAYLOAD + 64] = jnp.zeros((64, LANES), f32)
     for k in range(PLANES):
         block = HELD * jnp.concatenate([pert[c, :, k, :] for c in range(FIELDS - 1)], axis=0)
@@ -318,12 +320,15 @@
                 v0[k, jl, :, 128:256] = slab
 
             segments(
-                jnp.concatenate([last_field[k], halo[k * 96:(k + 1) * 96]], axis=0),
+                jnp.concatenate(
+                    [last_field[k], halo[k * EDGE:(k + 1) * EDGE], jnp.zeros((6, LANES), f32)],
+                    axis=0,
+                ),
                 hold.at[k], mid.at[k], store,
             )
         for q in range(3):
             coef[q, :, :, 0:128] = ct[q]
-            edge = halo[384 + q * 24:384 + q * 24 + HALO] * SCALES[q] + KEEPS[q]
+            edge = halo[COEFS + q * HALO:COEFS + (q + 1) * HALO] * SCALES[q] + KEEPS[q]
             block = jnp.concatenate(
                 [jnp.zeros((rows, LANES), f32)] + [edge] * FIELDS
                 + [jnp.zeros((128 - rows - FIELDS * HALO, LANES), f32)], axis=0,
@@ -361,7 +366,7 @@
                     )
         g = jnp.where(is_own, slot, jnp.where(halo_right == 1, slots + slot, slot))
         lanes_ref[0] = jnp.broadcast_to(cut_lanes(g), (8, LANES))
-        lanes_ref[1] = 2.0 * (own_flags + halo[456:464])
+        lanes_ref[1] = 2.0 * (own_flags + halo[FLAGS:PAYLOAD])
         lanes_ref[2] = 2.0 * (
             own_mirror + jnp.concatenate([jnp.zeros((8, 128), f32), far[56:64]], axis=1)
         )
@@ -434,7 +439,8 @@
                 r = (first[here] + first8[here]) + ca * (grad[here] + grad8[here])
                 r = r + partial[k, here]
                 r = r + zz[k, here] if k < 2 else r - zz[k - 2, here]
-                r = alpha * flat(v0[k, at:at + 8]) + beta * r
+                if not isinstance(alpha, float) or alpha:
+                    r = alpha * flat(v0[k, at:at + 8]) + beta * r
                 xs[k, 3 + at:11 + at] = r.reshape(8, SEGMENTS, LANES)
         n = depth * 8
         x = gs[3:3 + depth].reshape(n, LANES)
@@ -447,12 +453,23 @@
         z = couple_k(*split_small(s.reshape(n, LANES)))
         ca, cb, cd = (gcoef[q, 0:depth].reshape(n, LANES) for q in range(3))
         r = cb * e + cd * x - (first + first8) - ca * (grad + grad8) + z
-        gs[3:3 + depth] = alpha * gv[0:depth] + beta * r.reshape(depth, 8, LANES)
+        r = r.reshape(depth, 8, LANES)
+        if not isinstance(alpha, float) or alpha:
+            r = alpha * gv[0:depth] + beta * r
+        gs[3:3 + depth] = r
 
     def time_steps(depth):
+        weights = ((0.0, 1.0), (0.75, 0.25), (1.0 / 3.0, 2.0 / 3.0))
+        if second:
+            for alpha, beta in weights:
+                time_stage(depth, alpha, beta)
+            return
+
         def stage(s, carry):
-            alpha = jnp.where(s == 0, 0.0, jnp.where(s == 1, 0.75, 1.0 / 3.0)).astype(f32)
-            beta = jnp.where(s == 0, 1.0, jnp.where(s == 1, 0.25, 2.0 / 3.0)).astype(f32)
+            alpha, beta = (
+                jnp.where(s == 0, w[0], jnp.where(s == 1, w[1], w[2])).astype(f32)
+                for w in zip(*weights)
+            )
             time_stage(depth, alpha, beta)
             return carry
 

time: 47 us -> 46 us (0.979)
  Pallas kernels: 25.4 us -> 24.8 us
    pallas_call x1, Pallas kernels: 13.2 us -> 12.6 us  [on_device(): call(functools.partial(window_kernel, rows, total_rows, True), (shape(*pe...]
where the time goes in v4:
time: 46 us; the launch traced here: 45.8 us
  Pallas kernels  24.8 us (54%)
  starting transfers between devices  17.7 us (38%)
  waiting for transfers between devices  2.54 us (6%)
  local copies, waits for them, and re-layouts  0.64 us (1%)
    pallas_call x1, Pallas kernels, on_device(): call(functools.partial(window_kernel, rows, total_rows, True), (shape(*pe...  12.6 us
    ppermute x1, starting transfers between devices, on_device(): from_next = lax.ppermute(odd, 'wrap', next_chip)  8.8 us
    ppermute x1, starting transfers between devices, on_device(): strips = lax.ppermute(to_mirror, 'wrap', mirror)  8.76 us
    pallas_call x1, Pallas kernels, on_device(): call(functools.partial(window_kernel, rows, total_rows, False), (shape(*s...  6.3 us
    pallas_call x1, Pallas kernels, on_device(): call(functools.partial(prepare_kernel, rows), (payload, payload, shape(PL...  2.86 us
    pallas_call x1, Pallas kernels, on_device(): call(functools.partial(pack_mirror_kernel, rows), (shape(own + rows + 8,...  2.61 us
    ppermute x1, waiting for transfers between devices, on_device(): strips = lax.ppermute(to_mirror, 'wrap', mirror)  2.26 us
  transfers between devices with their start and end apart: 3, of which 2 were waited for; matrix products, arithmetic and copies ran while one was open for 0% of the time, Pallas kernels for 20%

profile of v4, /device:TPU:2, one launch (start us, length us, event | category | flops | bytes accessed | tf_op | source)
XLA Modules:
  0.0 45.8 jit_solution(14221530422239053419)
XLA Ops:
  0.0 0.0 copy-start
  0.0 0.0 copy-start.1
  0.0 0.0 copy-start.2
  0.0 0.0 copy-start.3
  0.0 0.0 copy-start.5
  0.0 0.0 copy-start.6
  0.0 2.6 %shard_map.91 = f32[200,128]{1,0:T(8,128)} custom-call(f32[5,32,4,256]{3,2,1,0:T(4,128)} %pert_hbm.3, f32[32,256]{1,0:T(8,128)} %ax_hbm.3, f32[32,256]{1,0:T(8,128)} %ae_hbm.3, f32[32,256]{1,0:T(8,128)} %sp_hbm.3, s32[1,32]{1,0:T(1,128)} %bitcast.2), custom_call_target="tpu_custom_call" | custom-call | flops 1000000000 | bytes 3000000 | tf_op jit(solution)/shard_map/pallas_call | solution.py:581
  2.7 0.0 copy-start.4
  2.7 8.8 %collective-permute-start = (f32[200,128]{1,0:T(8,128)}, f32[200,128]{1,0:T(8,128)S(1)}, u32[]{:S(2)}, u32[]{:S(2)}) collective-permute-start(f32[200,128]{1,0:T(8,128)} %shard_map.91), channel_id=1, source_target_pairs={{0,255},{1,254},{2,253},{3,252},{4,251},{5,250},{6,249},{7,248},{8... | collective-permute-start | bytes 307208 | tf_op jit(solution)/shard_map/ppermute | solution.py:593
  11.4 0.0 copy-start.7
  11.4 0.0 copy-start.8
  11.4 0.0 copy-done
  11.4 0.0 copy-done.1
  11.4 0.0 copy-done.2
  11.5 0.0 copy-done.3
  11.5 0.0 copy-done.5
  11.5 0.0 copy-done.6
  11.5 0.0 copy-done.4
  11.5 0.6 %copy-done.7 = s32[2]{0:T(128)S(1)} copy-done((s32[2]{0:T(128)S(1)}, s32[2]{0:T(128)}, u32[]{:S(2)}) %copy-start.7) | copy-done | bytes 32
  12.1 0.0 copy-done.8
  12.1 2.9 %shard_map.92 = (f32[488,256]{1,0:T(8,128)S(1)}, f32[488,256]{1,0:T(8,128)S(1)}, f32[4,32,8,128]{3,2,1,0:T(8,128)S(1)}, f32[3,32,8,128]{3,2,1,0:T(8,128)S(1)}, f...) custom-call(s32[1]{0:T(128)} %bitcast.me_ref, ...), custom_call_target="tpu_custom_call" | custom-call | flops 4000000000 | bytes 12000000 | tf_op jit(solution)/shard_map/pallas_call | solution.py:597
  15.0 2.3 %collective-permute-done.strips = f32[200,128]{1,0:T(8,128)S(1)} collective-permute-done((f32[200,128]{1,0:T(8,128)}, f32[200,128]{1,0:T(8,128)S(1)}, u32[]{:S(2)}, u32[]{:S(2)}) %collective-permute-start) | collective-permute-done | bytes 102432 | tf_op jit(solution)/shard_map/ppermute | solution.py:593
  17.2 0.4 shard_map.93
  17.6 0.1 collective-permute-start.2
  17.7 8.8 %collective-permute-start.1 = (f32[488,256]{1,0:T(8,128)S(1)}, f32[488,256]{1,0:T(8,128)S(1)}, u32[]{:S(2)}, u32[]{:S(2)}) collective-permute-start(f32[488,256]{1,0:T(8,128)S(1)} %get-tuple-element.28), channel_id=1, source_target_pairs={{1,2},{2,1},{3,4},{4,3},{5,6},{6,5},{7,8},{8,7},{9,10},{10,9},{11,... | collective-permute-start | bytes 1499144 | tf_op jit(solution)/shard_map/ppermute | solution.py:628
  26.6 0.0 collective-permute-done.2.halo_in
  26.6 6.3 %shard_map.94 = (f32[4,32,8,256]{3,2,1,0:T(8,128)S(1)}, f32[9,8,256]{2,1,0:T(8,128)S(1)}, f32[3,32,8,128]{3,2,1,0:T(8,128)S(1)}, f32[3,9,8,256]{3,2,1,0:T(8,128)S(1)}, f32[3,8,256]{2,1,0:T(8,128)S(1)}) custom-call(s32[1]{0:T(128)} %bitcast.me_ref, s32[1,32]{1,0:T(1,128)S(1)} %bitcast.4, f32[200,128]{1,0:T(8,128)S(1)} %collective-permute-done.strips, ...), custom_call_target="tpu_custom_call" | custom-call | flops 8000000000 | bytes 24000000 | tf_op jit(solution)/shard_map/pallas_call | solution.py:653
  32.9 0.3 collective-permute-done.1.halo_in
  33.1 12.6 %shard_map.95 = f32[5,32,4,256]{3,2,1,0:T(4,128)} custom-call(s32[1]{0:T(128)} %bitcast.me_ref, s32[1,32]{1,0:T(1,128)S(1)} %bitcast.5, f32[200,128]{1,0:T(8,128)S(1)} %collective-permute-done.strips, f32[4,32,8,128]{3,2,1,0:T(8,128)S(1)} %get-tuple-element.20.xt, f32[3,32,8,128]{3,2,1,0:T(8,128)S(1)} %get-tuple-element.21.ct, ...), custom_call_target="tpu_custom_call" | custom-call | flops 14000000000 | bytes 42000000 | tf_op jit(solution)/shard_map/pallas_call | solution.py:661
Async XLA Ops:
  0.0 11.4 %copy-start = (f32[5,32,4,256]{3,2,1,0:T(4,128)S(1)}, f32[5,32,4,256]{3,2,1,0:T(4,128)}, u32[]{:S(2)}) copy-start(f32[5,32,4,256]{3,2,1,0:T(4,128)} %pert_hbm.3) | copy-start | bytes 1966084
  0.0 11.4 %copy-start.1 = (f32[32,256]{1,0:T(8,128)S(1)}, f32[32,256]{1,0:T(8,128)}, u32[]{:S(2)}) copy-start(f32[32,256]{1,0:T(8,128)} %ax_hbm.3) | copy-start | bytes 98308
  0.0 11.4 %copy-start.2 = (f32[32,256]{1,0:T(8,128)S(1)}, f32[32,256]{1,0:T(8,128)}, u32[]{:S(2)}) copy-start(f32[32,256]{1,0:T(8,128)} %ae_hbm.3) | copy-start | bytes 98308
  0.0 11.4 %copy-start.3 = (f32[32,256]{1,0:T(8,128)S(1)}, f32[32,256]{1,0:T(8,128)}, u32[]{:S(2)}) copy-start(f32[32,256]{1,0:T(8,128)} %sp_hbm.3) | copy-start | bytes 98308
  0.0 11.4 %copy-start.5 = (f32[5,5]{1,0:T(8,128)S(1)}, f32[5,5]{1,0:T(8,128)}, u32[]{:S(2)}) copy-start(f32[5,5]{1,0:T(8,128)} %ceta.1) | copy-start | bytes 304
  0.0 11.4 %copy-start.6 = (f32[5,5]{1,0:T(8,128)S(1)}, f32[5,5]{1,0:T(8,128)}, u32[]{:S(2)}) copy-start(f32[5,5]{1,0:T(8,128)} %cspan.1) | copy-start | bytes 304
  2.7 8.8 %copy-start.4 = (f32[5,5]{1,0:T(8,128)S(1)}, f32[5,5]{1,0:T(8,128)}, u32[]{:S(2)}) copy-start(f32[5,5]{1,0:T(8,128)} %cxi.1) | copy-start | bytes 304
  2.7 14.6 %collective-permute-start = (f32[200,128]{1,0:T(8,128)}, f32[200,128]{1,0:T(8,128)S(1)}, u32[]{:S(2)}, u32[]{:S(2)}) collective-permute-start(f32[200,128]{1,0:T(8,128)} %shard_map.91), channel_id=1, source_target_pairs={{0,255},{1,254},{2,253},{3,252},{4,251},{5,250},{6,249},{7,248},{8... | collective-permute-start | bytes 307208 | tf_op jit(solution)/shard_map/ppermute | solution.py:593
  11.4 0.7 %copy-start.7 = (s32[2]{0:T(128)S(1)}, s32[2]{0:T(128)}, u32[]{:S(2)}) copy-start(s32[2]{0:T(128)} %cut_ref.1) | copy-start | bytes 28
  11.4 0.7 %copy-start.8 = (s32[32]{0:T(128)S(1)}, s32[32]{0:T(128)}, u32[]{:S(2)}) copy-start(s32[32]{0:T(128)} %param.17) | copy-start | bytes 388
  17.6 8.9 %collective-permute-start.2 = (f32[488,256]{1,0:T(8,128)S(1)}, f32[488,256]{1,0:T(8,128)S(1)}, u32[]{:S(2)}, u32[]{:S(2)}) collective-permute-start(f32[488,256]{1,0:T(8,128)S(1)} %get-tuple-element.29), channel_id=1, source_target_pairs={{0,1},{1,0},{2,3},{3,2},{4,5},{5,4},{6,7},{7,6},{8,9},{9,8},{10,11... | collective-permute-start | bytes 1499144 | tf_op jit(solution)/shard_map/ppermute | solution.py:629
  17.7 15.4 %collective-permute-start.1 = (f32[488,256]{1,0:T(8,128)S(1)}, f32[488,256]{1,0:T(8,128)S(1)}, u32[]{:S(2)}, u32[]{:S(2)}) collective-permute-start(f32[488,256]{1,0:T(8,128)S(1)} %get-tuple-element.28), channel_id=1, source_target_pairs={{1,2},{2,1},{3,4},{4,3},{5,6},{6,5},{7,8},{8,7},{9,10},{10,9},{11,... | collective-permute-start | bytes 1499144 | tf_op jit(solution)/shard_map/ppermute | solution.py:628

commit v5 on v4

--- a/solution.py
+++ b/solution.py
@@ -442,6 +442,8 @@
                 if not isinstance(alpha, float) or alpha:
                     r = alpha * flat(v0[k, at:at + 8]) + beta * r
                 xs[k, 3 + at:11 + at] = r.reshape(8, SEGMENTS, LANES)
+        if not depth:
+            return
         n = depth * 8
         x = gs[3:3 + depth].reshape(n, LANES)
         e = slopes(lambda at: gs[at:at + depth], 3).reshape(n, LANES)
@@ -461,8 +463,8 @@
     def time_steps(depth):
         weights = ((0.0, 1.0), (0.75, 0.25), (1.0 / 3.0, 2.0 / 3.0))
         if second:
-            for alpha, beta in weights:
-                time_stage(depth, alpha, beta)
+            for n, (alpha, beta) in enumerate(weights):
+                time_stage(-(-(depth - 3 * n) // 4) * 4, alpha, beta)
             return
 
         def stage(s, carry):
@@ -500,7 +502,7 @@
         set_xi_weights(0, HALO)
 
     read_window(halo_in, is_odd)
-    time_steps(HALO - 2)
+    time_steps(HALO - 3)
     @pl.when(outside)
     def _():
         set_xi_weights(jnp.where(at_start, REACH, 0), jnp.where(at_start, HALO, REACH))
@@ -520,7 +522,7 @@
     lanes_ref[0] = jnp.broadcast_to(cut_lanes(g), (8, LANES))
     lanes_ref[1] = jnp.where(from_e, le[1], lanes_ref[1])
     lanes_ref[2] = jnp.where(from_e, le[2], lanes_ref[2])
-    time_steps(REACH - 1)
+    time_steps(REACH - 3)
     for k in range(PLANES):
         block = from_segments(
             lambda jl: xs[k, 3 + jl, :, 0:128], hold.at[k], mid.at[k]

time: 46 us -> 46 us (level)
  no operation moved by 1% of the time
where the time goes in v5:
time: 46 us; the launch traced here: 45.8 us
  Pallas kernels  24.8 us (54%)
  starting transfers between devices  17.7 us (38%)
  waiting for transfers between devices  2.54 us (6%)
  local copies, waits for them, and re-layouts  0.64 us (1%)
    pallas_call x1, Pallas kernels, on_device(): call(functools.partial(window_kernel, rows, total_rows, True), (shape(*pe...  12.7 us
    ppermute x1, starting transfers between devices, on_device(): from_next = lax.ppermute(odd, 'wrap', next_chip)  8.8 us
    ppermute x1, starting transfers between devices, on_device(): strips = lax.ppermute(to_mirror, 'wrap', mirror)  8.76 us
    pallas_call x1, Pallas kernels, on_device(): call(functools.partial(window_kernel, rows, total_rows, False), (shape(*s...  6.3 us
    pallas_call x1, Pallas kernels, on_device(): call(functools.partial(prepare_kernel, rows), (payload, payload, shape(PL...  2.86 us
    pallas_call x1, Pallas kernels, on_device(): call(functools.partial(pack_mirror_kernel, rows), (shape(own + rows + 8,...  2.61 us
    ppermute x1, waiting for transfers between devices, on_device(): strips = lax.ppermute(to_mirror, 'wrap', mirror)  2.26 us
  transfers between devices with their start and end apart: 3, of which 2 were waited for; matrix products, arithmetic and copies ran while one was open for 0% of the time, Pallas kernels for 20%

profile of v5, /device:TPU:2, one launch (start us, length us, event | category | flops | bytes accessed | tf_op | source)
XLA Modules:
  0.0 45.8 jit_solution(4514685949484477656)
XLA Ops:
  0.0 0.0 copy-start
  0.0 0.0 copy-start.1
  0.0 0.0 copy-start.2
  0.0 0.0 copy-start.3
  0.0 0.0 copy-start.5
  0.0 0.0 copy-start.6
  0.0 2.6 %shard_map.91 = f32[200,128]{1,0:T(8,128)} custom-call(f32[5,32,4,256]{3,2,1,0:T(4,128)} %pert_hbm.3, f32[32,256]{1,0:T(8,128)} %ax_hbm.3, f32[32,256]{1,0:T(8,128)} %ae_hbm.3, f32[32,256]{1,0:T(8,128)} %sp_hbm.3, s32[1,32]{1,0:T(1,128)} %bitcast.2), custom_call_target="tpu_custom_call" | custom-call | flops 1000000000 | bytes 3000000 | tf_op jit(solution)/shard_map/pallas_call | solution.py:583
  2.7 0.0 copy-start.4
  2.7 8.8 %collective-permute-start = (f32[200,128]{1,0:T(8,128)}, f32[200,128]{1,0:T(8,128)S(1)}, u32[]{:S(2)}, u32[]{:S(2)}) collective-permute-start(f32[200,128]{1,0:T(8,128)} %shard_map.91), channel_id=1, source_target_pairs={{0,255},{1,254},{2,253},{3,252},{4,251},{5,250},{6,249},{7,248},{8... | collective-permute-start | bytes 307208 | tf_op jit(solution)/shard_map/ppermute | solution.py:595
  11.4 0.0 copy-start.7
  11.4 0.0 copy-start.8
  11.4 0.0 copy-done
  11.4 0.0 copy-done.1
  11.4 0.0 copy-done.2
  11.5 0.0 copy-done.3
  11.5 0.0 copy-done.5
  11.5 0.0 copy-done.6
  11.5 0.0 copy-done.4
  11.5 0.6 %copy-done.7 = s32[2]{0:T(128)S(1)} copy-done((s32[2]{0:T(128)S(1)}, s32[2]{0:T(128)}, u32[]{:S(2)}) %copy-start.7) | copy-done | bytes 32
  12.1 0.0 copy-done.8
  12.1 2.9 %shard_map.92 = (f32[488,256]{1,0:T(8,128)S(1)}, f32[488,256]{1,0:T(8,128)S(1)}, f32[4,32,8,128]{3,2,1,0:T(8,128)S(1)}, f32[3,32,8,128]{3,2,1,0:T(8,128)S(1)}, f...) custom-call(s32[1]{0:T(128)} %bitcast.me_ref, ...), custom_call_target="tpu_custom_call" | custom-call | flops 4000000000 | bytes 12000000 | tf_op jit(solution)/shard_map/pallas_call | solution.py:599
  15.0 2.3 %collective-permute-done.strips = f32[200,128]{1,0:T(8,128)S(1)} collective-permute-done((f32[200,128]{1,0:T(8,128)}, f32[200,128]{1,0:T(8,128)S(1)}, u32[]{:S(2)}, u32[]{:S(2)}) %collective-permute-start) | collective-permute-done | bytes 102432 | tf_op jit(solution)/shard_map/ppermute | solution.py:595
  17.2 0.4 shard_map.93
  17.6 0.1 collective-permute-start.2
  17.7 8.8 %collective-permute-start.1 = (f32[488,256]{1,0:T(8,128)S(1)}, f32[488,256]{1,0:T(8,128)S(1)}, u32[]{:S(2)}, u32[]{:S(2)}) collective-permute-start(f32[488,256]{1,0:T(8,128)S(1)} %get-tuple-element.28), channel_id=1, source_target_pairs={{1,2},{2,1},{3,4},{4,3},{5,6},{6,5},{7,8},{8,7},{9,10},{10,9},{11,... | collective-permute-start | bytes 1499144 | tf_op jit(solution)/shard_map/ppermute | solution.py:630
  26.6 0.0 collective-permute-done.2.halo_in
  26.6 6.3 %shard_map.94 = (f32[4,32,8,256]{3,2,1,0:T(8,128)S(1)}, f32[9,8,256]{2,1,0:T(8,128)S(1)}, f32[3,32,8,128]{3,2,1,0:T(8,128)S(1)}, f32[3,9,8,256]{3,2,1,0:T(8,128)S(1)}, f32[3,8,256]{2,1,0:T(8,128)S(1)}) custom-call(s32[1]{0:T(128)} %bitcast.me_ref, s32[1,32]{1,0:T(1,128)S(1)} %bitcast.4, f32[200,128]{1,0:T(8,128)S(1)} %collective-permute-done.strips, ...), custom_call_target="tpu_custom_call" | custom-call | flops 8000000000 | bytes 24000000 | tf_op jit(solution)/shard_map/pallas_call | solution.py:655
  32.9 0.3 collective-permute-done.1.halo_in
  33.1 12.7 %shard_map.95 = f32[5,32,4,256]{3,2,1,0:T(4,128)} custom-call(s32[1]{0:T(128)} %bitcast.me_ref, s32[1,32]{1,0:T(1,128)S(1)} %bitcast.5, f32[200,128]{1,0:T(8,128)S(1)} %collective-permute-done.strips, f32[4,32,8,128]{3,2,1,0:T(8,128)S(1)} %get-tuple-element.20.xt, f32[3,32,8,128]{3,2,1,0:T(8,128)S(1)} %get-tuple-element.21.ct, ...), custom_call_target="tpu_custom_call" | custom-call | flops 14000000000 | bytes 42000000 | tf_op jit(solution)/shard_map/pallas_call | solution.py:663
Async XLA Ops:
  0.0 11.4 %copy-start = (f32[5,32,4,256]{3,2,1,0:T(4,128)S(1)}, f32[5,32,4,256]{3,2,1,0:T(4,128)}, u32[]{:S(2)}) copy-start(f32[5,32,4,256]{3,2,1,0:T(4,128)} %pert_hbm.3) | copy-start | bytes 1966084
  0.0 11.4 %copy-start.1 = (f32[32,256]{1,0:T(8,128)S(1)}, f32[32,256]{1,0:T(8,128)}, u32[]{:S(2)}) copy-start(f32[32,256]{1,0:T(8,128)} %ax_hbm.3) | copy-start | bytes 98308
  0.0 11.4 %copy-start.2 = (f32[32,256]{1,0:T(8,128)S(1)}, f32[32,256]{1,0:T(8,128)}, u32[]{:S(2)}) copy-start(f32[32,256]{1,0:T(8,128)} %ae_hbm.3) | copy-start | bytes 98308
  0.0 11.4 %copy-start.3 = (f32[32,256]{1,0:T(8,128)S(1)}, f32[32,256]{1,0:T(8,128)}, u32[]{:S(2)}) copy-start(f32[32,256]{1,0:T(8,128)} %sp_hbm.3) | copy-start | bytes 98308
  0.0 11.4 %copy-start.5 = (f32[5,5]{1,0:T(8,128)S(1)}, f32[5,5]{1,0:T(8,128)}, u32[]{:S(2)}) copy-start(f32[5,5]{1,0:T(8,128)} %ceta.1) | copy-start | bytes 304
  0.0 11.4 %copy-start.6 = (f32[5,5]{1,0:T(8,128)S(1)}, f32[5,5]{1,0:T(8,128)}, u32[]{:S(2)}) copy-start(f32[5,5]{1,0:T(8,128)} %cspan.1) | copy-start | bytes 304
  2.7 8.8 %copy-start.4 = (f32[5,5]{1,0:T(8,128)S(1)}, f32[5,5]{1,0:T(8,128)}, u32[]{:S(2)}) copy-start(f32[5,5]{1,0:T(8,128)} %cxi.1) | copy-start | bytes 304
  2.7 14.6 %collective-permute-start = (f32[200,128]{1,0:T(8,128)}, f32[200,128]{1,0:T(8,128)S(1)}, u32[]{:S(2)}, u32[]{:S(2)}) collective-permute-start(f32[200,128]{1,0:T(8,128)} %shard_map.91), channel_id=1, source_target_pairs={{0,255},{1,254},{2,253},{3,252},{4,251},{5,250},{6,249},{7,248},{8... | collective-permute-start | bytes 307208 | tf_op jit(solution)/shard_map/ppermute | solution.py:595
  11.4 0.7 %copy-start.7 = (s32[2]{0:T(128)S(1)}, s32[2]{0:T(128)}, u32[]{:S(2)}) copy-start(s32[2]{0:T(128)} %cut_ref.1) | copy-start | bytes 28
  11.4 0.7 %copy-start.8 = (s32[32]{0:T(128)S(1)}, s32[32]{0:T(128)}, u32[]{:S(2)}) copy-start(s32[32]{0:T(128)} %param.17) | copy-start | bytes 388
  17.6 8.9 %collective-permute-start.2 = (f32[488,256]{1,0:T(8,128)S(1)}, f32[488,256]{1,0:T(8,128)S(1)}, u32[]{:S(2)}, u32[]{:S(2)}) collective-permute-start(f32[488,256]{1,0:T(8,128)S(1)} %get-tuple-element.29), channel_id=1, source_target_pairs={{0,1},{1,0},{2,3},{3,2},{4,5},{5,4},{6,7},{7,6},{8,9},{9,8},{10,11... | collective-permute-start | bytes 1499144 | tf_op jit(solution)/shard_map/ppermute | solution.py:631
  17.7 15.4 %collective-permute-start.1 = (f32[488,256]{1,0:T(8,128)S(1)}, f32[488,256]{1,0:T(8,128)S(1)}, u32[]{:S(2)}, u32[]{:S(2)}) collective-permute-start(f32[488,256]{1,0:T(8,128)S(1)} %get-tuple-element.28), channel_id=1, source_target_pairs={{1,2},{2,1},{3,4},{4,3},{5,6},{6,5},{7,8},{8,7},{9,10},{10,9},{11,... | collective-permute-start | bytes 1499144 | tf_op jit(solution)/shard_map/ppermute | solution.py:630
